TPU v7x, 32 devices: a whole 2x2x4 slice. The times are simulated.
32 devices in a mesh: fsdp: 32 (over z, y, x, core).
Axes of the slice: x: 2, y: 2, z: 4, core: 2. Of those that a mesh axis runs over, the one named last changes fastest.
Arguments:
- tokens: bfloat16 [16384, 896], P('fsdp'), may hold values from -6 to 6
- lengths: int32 [48], replicated, may hold values from 1 to 512, 16384 in all
- gains: bfloat16 [1792], P('fsdp'), may hold values from 0.5 to 1.5
- w_qkv: bfloat16 [1032192], P('fsdp'), may hold values from -0.1875 to 0.1875
- b_qkv: bfloat16 [1152], P('fsdp'), may hold values from -3 to 3
- w_out: bfloat16 [802816], P('fsdp'), may hold values from -0.75 to 0.75
- w_gate_up: bfloat16 [8716288], P('fsdp'), may hold values from -0.1875 to 0.1875
- w_down: bfloat16 [4358144], P('fsdp'), may hold values from -0.078125 to 0.078125
- grad_out: bfloat16 [16384, 896], P('fsdp'), may hold values from -6 to 6
Outputs:
- output: bfloat16 [16384, 896], P('fsdp')
- grad_tokens: float32 [16384, 896], P('fsdp')
- grad_gains: float32 [1792], P('fsdp')
- grad_w_qkv: float32 [1032192], P('fsdp')
- grad_b_qkv: float32 [1152], P('fsdp')
- grad_w_out: float32 [802816], P('fsdp')
- grad_w_gate_up: float32 [8716288], P('fsdp')
- grad_w_down: float32 [4358144], P('fsdp')
Inputs may be any that keep to these rules, and one draw needn't show every extreme that they name: Sequences lie end to end in order; the lengths sum to 16384 and the longest has exactly 512 tokens.
All inputs are finite; a program needn't handle non-finite values.
Results may differ from a plain program's by a relative error of at most 0.011.
Values may be sent and summed in bfloat16 or wider, within the bound.
A program may use at most 256 MiB of HBM per device.

v0:
```python
import math

import jax
import jax.numpy as jnp
from jax import lax
from jax.sharding import PartitionSpec as P

FF = 4864
HEADS = 14
KV_HEADS = 2
HD = 64
QKV = 1152


EPSILON = 1e-06
ROPE_BASE = 1000000.0
MASKED_SCORE = -1e30


def passed_along(x, axis, by):
    peers = lax.axis_size(axis)
    pairs = [(i, i + by) for i in range(peers) if 0 <= i + by < peers]
    return lax.ppermute(x, axis, pairs)


def rope_tables(positions, head_dim):
    half_dim = head_dim // 2
    frequency = ROPE_BASE ** (-(2.0 * jnp.arange(half_dim, dtype=jnp.float32)) / head_dim)
    angles = positions.astype(jnp.float32)[:, None] * frequency[None, :]
    angles = jnp.concatenate([angles, angles], axis=1)
    return (jnp.cos(angles)[:, None, :], jnp.sin(angles)[:, None, :])


def turn_half(values):
    half_dim = values.shape[-1] // 2
    return jnp.concatenate([-values[..., half_dim:], values[..., :half_dim]], axis=-1)


def rotate(values, cosine, sine):
    return values * cosine + turn_half(values) * sine


def unrotate(values, cosine, sine):
    return values * cosine - turn_half(values) * sine


def segment_info(lengths, base_index, count):
    token_index = base_index + jnp.arange(count, dtype=jnp.int32)
    ends = jnp.cumsum(lengths, dtype=jnp.int32)
    before = ends[None, :] <= token_index[:, None]
    segment = jnp.sum(before.astype(jnp.int32), axis=1, dtype=jnp.int32)
    start_of = jnp.sum(jnp.where(before, lengths[None, :], 0), axis=1, dtype=jnp.int32)
    return (token_index, segment, token_index - start_of)


def outer_sum(left, right):
    return lax.dot_general(
        left, right, (((0,), (0,)), ((), ())), preferred_element_type=jnp.float32
    )


def back_dot(left, right):
    return lax.dot_general(
        left, right, (((1,), (1,)), ((), ())), preferred_element_type=jnp.float32
    )


def unpack_attention(params, width):
    full_gains, qkv_flat, bias_flat, out_flat = params
    return (
        full_gains[:width].astype(jnp.float32),
        full_gains[width:].astype(jnp.float32),
        qkv_flat.reshape(width, QKV),
        bias_flat[:QKV].astype(jnp.float32),
        out_flat.reshape(HEADS * HD, width),
    )


def unpack_mlp(params, width):
    gu_flat, down_flat = params
    return (gu_flat.reshape(width, 2 * FF), down_flat.reshape(FF, width))


def norm_back(grad_normed, hidden, factor, gain):
    normed = hidden * factor
    grad_gain = jnp.sum(grad_normed * normed, axis=0)
    scaled = grad_normed * gain
    grad_hidden = factor * scaled - normed * factor * jnp.mean(
        scaled * normed, axis=1, keepdims=True
    )
    return (grad_hidden, grad_gain)


def local(tokens, lengths, gains, w_qkv, b_qkv, w_out, w_gate_up, w_down, grad_out):
    tok_rows = tokens.shape[0]
    width = tokens.shape[1]
    n_devices = lax.axis_size("fsdp")
    query_dim = HEADS * HD
    kv_dim = KV_HEADS * HD
    groups = HEADS // KV_HEADS
    scale = 1.0 / math.sqrt(HD)
    block_rows = min(tok_rows, 512)
    block_count = tok_rows // block_rows
    attn_params = (
        lax.all_gather(gains, "fsdp", axis=0, tiled=True),
        lax.all_gather(w_qkv, "fsdp", axis=0, tiled=True),
        lax.all_gather(b_qkv, "fsdp", axis=0, tiled=True),
        lax.all_gather(w_out, "fsdp", axis=0, tiled=True),
    )
    mlp_params = (
        lax.all_gather(w_gate_up, "fsdp", axis=0, tiled=True),
        lax.all_gather(w_down, "fsdp", axis=0, tiled=True),
    )
    gain_one, gain_two, wqkv, bias, wout = unpack_attention(attn_params, width)
    wgu, wdown = unpack_mlp(mlp_params, width)
    base_index = lax.axis_index("fsdp") * tok_rows
    token_index, segment, position = segment_info(lengths, base_index, tok_rows)
    prev_index, prev_segment, unused_pos = segment_info(lengths, base_index - tok_rows, tok_rows)
    key_index = jnp.concatenate([prev_index, token_index])
    key_segment = jnp.concatenate([prev_segment, segment])
    hidden = tokens.astype(jnp.float32)
    factor_one = lax.rsqrt(jnp.mean(hidden * hidden, axis=1, keepdims=True) + EPSILON)
    normed_one = (hidden * factor_one * gain_one).astype(jnp.bfloat16)
    linear = jnp.dot(normed_one, wqkv, preferred_element_type=jnp.float32) + bias
    cosine, sine = rope_tables(position, HD)
    query = rotate(linear[:, :query_dim].reshape(tok_rows, HEADS, HD), cosine, sine).astype(
        jnp.bfloat16
    )
    keyed = rotate(
        linear[:, query_dim : query_dim + kv_dim].reshape(tok_rows, KV_HEADS, HD), cosine, sine
    )
    keyed = keyed.astype(jnp.bfloat16).reshape(tok_rows, kv_dim)
    valued = linear[:, query_dim + kv_dim :].astype(jnp.bfloat16)
    key_prev, value_prev = passed_along((keyed, valued), "fsdp", 1)
    key_all = jnp.concatenate([key_prev, keyed]).reshape(2 * tok_rows, KV_HEADS, HD)
    value_all = jnp.concatenate([value_prev, valued]).reshape(2 * tok_rows, KV_HEADS, HD)
    query_four = query.reshape(tok_rows, KV_HEADS, groups, HD)

    def scores_of():
        allowed = (
            (key_segment[None, :] == segment[:, None])
            & (key_index[None, :] <= token_index[:, None])
            & (key_index[None, :] >= 0)
        )
        scores = (
            jnp.einsum("qkgd,jkd->kgqj", query_four, key_all, preferred_element_type=jnp.float32)
            * scale
        )
        scores = jnp.where(allowed[None, None], scores, MASKED_SCORE)
        return (query_four, key_all, value_all, scores)

    def attend(number):
        rows_q, key_block, value_block, scores = scores_of()
        row_max = jnp.max(scores, axis=-1, keepdims=True)
        weight = jnp.exp(scores - row_max)
        row_sum = jnp.sum(weight, axis=-1, keepdims=True)
        probs = (weight / row_sum).astype(jnp.bfloat16)
        mixed = jnp.einsum("kgqj,jkd->qkgd", probs, value_block, preferred_element_type=jnp.float32)
        return (mixed.reshape(block_rows, query_dim), row_max + jnp.log(row_sum))

    mixed_blocks, log_sums = lax.map(attend, jnp.arange(block_count, dtype=jnp.int32))
    attended = mixed_blocks.reshape(tok_rows, query_dim).astype(jnp.bfloat16)
    middle = hidden + jnp.dot(attended, wout, preferred_element_type=jnp.float32)
    factor_two = lax.rsqrt(jnp.mean(middle * middle, axis=1, keepdims=True) + EPSILON)
    normed_two = (middle * factor_two * gain_two).astype(jnp.bfloat16)
    gate_up = jnp.dot(normed_two, wgu, preferred_element_type=jnp.float32)
    gate_pre = gate_up[:, :FF]
    up_pre = gate_up[:, FF:]
    sigma = jax.nn.sigmoid(gate_pre)
    silu_gate = gate_pre * sigma
    product = (silu_gate * up_pre).astype(jnp.bfloat16)
    output = (middle + jnp.dot(product, wdown, preferred_element_type=jnp.float32)).astype(
        jnp.bfloat16
    )
    back_mlp = (
        lax.all_gather(w_gate_up, "fsdp", axis=0, tiled=True),
        lax.all_gather(w_down, "fsdp", axis=0, tiled=True),
    )
    back_attn = (
        lax.all_gather(gains, "fsdp", axis=0, tiled=True),
        lax.all_gather(w_qkv, "fsdp", axis=0, tiled=True),
        lax.all_gather(b_qkv, "fsdp", axis=0, tiled=True),
        lax.all_gather(w_out, "fsdp", axis=0, tiled=True),
    )
    gain_one_b, gain_two_b, wqkv_b, unused_bias, wout_b = unpack_attention(back_attn, width)
    wgu_b, wdown_b = unpack_mlp(back_mlp, width)
    grad_down = outer_sum(product, grad_out)
    grad_product = back_dot(grad_out, wdown_b)
    grad_gate = grad_product * up_pre * sigma * (1.0 + gate_pre * (1.0 - sigma))
    grad_up = grad_product * silu_gate
    grad_gu = jnp.concatenate([grad_gate, grad_up], axis=1).astype(jnp.bfloat16)
    grad_wgu = outer_sum(normed_two, grad_gu)
    mlp_grads = (
        lax.psum_scatter(grad_wgu.reshape(n_devices, -1), "fsdp", scatter_dimension=0, tiled=True),
        lax.psum_scatter(grad_down.reshape(n_devices, -1), "fsdp", scatter_dimension=0, tiled=True),
    )
    grad_normed_two = back_dot(grad_gu, wgu_b)
    grad_middle_norm, grad_gain_two = norm_back(grad_normed_two, middle, factor_two, gain_two_b)
    grad_middle = grad_out.astype(jnp.float32) + grad_middle_norm
    grad_branch = grad_middle.astype(jnp.bfloat16)
    grad_wout = outer_sum(attended, grad_branch)
    grad_att = back_dot(grad_branch, wout_b).astype(jnp.bfloat16)
    grad_att_four = grad_att.reshape(tok_rows, KV_HEADS, groups, HD)

    def back_block(number, carried):
        grad_query, grad_key, grad_value = carried
        rows_q, key_block, value_block, scores = scores_of()
        probs = jnp.exp(scores - log_sums[number])
        grad_probs = jnp.einsum(
            "qkgd,jkd->kgqj", grad_att_four, value_block, preferred_element_type=jnp.float32
        )
        inner = jnp.sum(probs * grad_probs, axis=-1, keepdims=True)
        grad_scores = (probs * (grad_probs - inner)).astype(jnp.bfloat16)
        part_query = (
            jnp.einsum("kgqj,jkd->qkgd", grad_scores, key_block, preferred_element_type=jnp.float32)
            * scale
        )
        part_key = (
            jnp.einsum("kgqj,qkgd->jkd", grad_scores, rows_q, preferred_element_type=jnp.float32)
            * scale
        )
        part_value = jnp.einsum(
            "kgqj,qkgd->jkd",
            probs.astype(jnp.bfloat16),
            grad_att_four,
            preferred_element_type=jnp.float32,
        )
        grad_query = part_query
        grad_key = grad_key + part_key
        grad_value = grad_value + part_value
        return (grad_query, grad_key, grad_value)

    start_state = (
        jnp.zeros((tok_rows, KV_HEADS, groups, HD), jnp.float32),
        jnp.zeros((2 * tok_rows, KV_HEADS, HD), jnp.float32),
        jnp.zeros((2 * tok_rows, KV_HEADS, HD), jnp.float32),
    )
    grad_query, grad_key, grad_value = lax.fori_loop(0, block_count, back_block, start_state)
    key_back, value_back = (
        passed_along(grad_key[:tok_rows].astype(jnp.bfloat16), "fsdp", -1).astype(jnp.float32),
        passed_along(grad_value[:tok_rows].astype(jnp.bfloat16), "fsdp", -1).astype(jnp.float32),
    )
    grad_key_own = grad_key[tok_rows:] + key_back
    grad_value_own = (grad_value[tok_rows:] + value_back).reshape(tok_rows, kv_dim)
    grad_query_lin = unrotate(grad_query.reshape(tok_rows, HEADS, HD), cosine, sine).reshape(
        tok_rows, query_dim
    )
    grad_key_lin = unrotate(grad_key_own, cosine, sine).reshape(tok_rows, kv_dim)
    grad_linear = jnp.concatenate([grad_query_lin, grad_key_lin, grad_value_own], axis=1).astype(
        jnp.bfloat16
    )
    grad_wqkv = outer_sum(normed_one, grad_linear)
    grad_bias = jnp.sum(grad_linear.astype(jnp.float32), axis=0)
    grad_normed_one = back_dot(grad_linear, wqkv_b)
    grad_hidden_norm, grad_gain_one = norm_back(grad_normed_one, hidden, factor_one, gain_one_b)
    grad_tokens = grad_middle + grad_hidden_norm
    bias_full = b_qkv.shape[0] * n_devices
    grad_bias_full = jnp.concatenate([grad_bias, jnp.zeros((bias_full - QKV,), jnp.float32)])
    grad_gains_full = jnp.concatenate([grad_gain_one, grad_gain_two])
    attn_grads = (
        lax.psum_scatter(
            grad_gains_full.reshape(n_devices, -1), "fsdp", scatter_dimension=0, tiled=True
        ),
        lax.psum_scatter(grad_wqkv.reshape(n_devices, -1), "fsdp", scatter_dimension=0, tiled=True),
        lax.psum_scatter(
            grad_bias_full.reshape(n_devices, -1), "fsdp", scatter_dimension=0, tiled=True
        ),
        lax.psum_scatter(grad_wout.reshape(n_devices, -1), "fsdp", scatter_dimension=0, tiled=True),
    )
    return (
        output,
        grad_tokens,
        attn_grads[0].reshape(-1),
        attn_grads[1].reshape(-1),
        attn_grads[2].reshape(-1),
        attn_grads[3].reshape(-1),
        mlp_grads[0].reshape(-1),
        mlp_grads[1].reshape(-1),
    )


def solution(mesh):
    in_specs = (
        P("fsdp", None),
        P(),
        P("fsdp"),
        P("fsdp"),
        P("fsdp"),
        P("fsdp"),
        P("fsdp"),
        P("fsdp"),
        P("fsdp", None),
    )
    out_specs = (
        P("fsdp", None),
        P("fsdp", None),
        P("fsdp"),
        P("fsdp"),
        P("fsdp"),
        P("fsdp"),
        P("fsdp"),
        P("fsdp"),
    )
    return jax.shard_map(local, mesh=mesh, in_specs=in_specs, out_specs=out_specs, check_vma=False)
```

profile of v0, /device:TPU:0, one launch (start us, length us, event | category | flops | bytes accessed | tf_op | source)
XLA Modules:
  0.0 1491.2 jit_solution(14254541646528019982)
XLA Ops:
  13.5 42.3 %all-reduce.10 = (bf16[1152]{0:T(1024)(128)(2,1)S(1)}, bf16[1792]{0:T(1024)(128)(2,1)S(1)}) all-reduce(bf16[1152]{0:T(1024)(128)(2,1)S(1)} %dynamic-update-slice.1, bf16[1792]{0:T(1024)(128)(2,1)S(1)} %dynamic-update-slice), channel_id=1, replica_groups=mesh['fsdp'=32] {'fsdp'}, use_global_device_ids=true, to_apply=%add.1 | all-reduce | flops 2944 | bytes 11776
  60.1 13.3 all-gather.13.cloned.1.call-done
  73.4 10.8 reduce.2
  84.2 3.6 reshape.348
  87.8 49.8 %all-gather.11.cloned.1.call-done = bf16[32,1,32256]{2,1,0:T(2,128)(2,1)} async-done(((bf16[1,1,32256]{2,1,0:T(2,128)(2,1)}), bf16[32,1,32256]{2,1,0:T(2,128)(2,1)}) %all-gather.11.cloned.1.call-update) | async-done | bytes 2064400 | tf_op jit(solution)/shard_map/all_gather | solution.py:106
  137.6 12.2 reduce
  149.8 4.1 reshape.341
  173.7 12.3 fusion.54
  186.0 12.6 fusion.3
  198.7 12.6 fusion.27
  212.8 6.5 all-gather.9.cloned.1.call-done
  219.2 16.4 %reshape.350 = bf16[4864,896]{1,0:T(8,128)(2,1)} reshape(bf16[4358144]{0:T(1024)(128)(2,1)} %all-gather.9.cloned.1.call-done) | data formatting | bytes 17432576 | tf_op jit(solution)/shard_map/reshape | solution.py:81
  235.7 102.9 %all-gather.7.cloned.1.call-done = bf16[8716288]{0:T(1024)(128)(2,1)} async-done(((bf16[272384]{0:T(1024)(128)(2,1)}), bf16[8716288]{0:T(1024)(128)(2,1)}) %all-gather.7.cloned.1.call-update) | async-done | bytes 17432592 | tf_op jit(solution)/shard_map/all_gather | solution.py:111
  338.6 29.9 %reshape.349 = bf16[896,9728]{1,0:T(8,128)(2,1)} reshape(bf16[8716288]{0:T(1024)(128)(2,1)} %all-gather.7.cloned.1.call-done) | data formatting | bytes 34865152 | tf_op jit(solution)/shard_map/reshape | solution.py:81
  368.5 18.3 %fusion.52 = f32[512,9728]{1,0:T(8,128)} fusion(bf16[896,9728]{1,0:T(8,128)(2,1)} %reshape.349, f32[512,896]{1,0:T(8,128)S(1)} %get-tuple-element.112, f32[896]{0:T(1024)S(1)} %get-tuple-element.107, f32[512]{0:T(512)S(1)} %add_rsqrt_fusion), kind=kOutput, calls=%fused_computation.117 | convolution fusion | flops 8926855168 | bytes 39196160 | tf_op jit(solution)/shard_map/dot_general | solution.py:166
  386.7 19.0 %multiply_convert_fusion.1 = (bf16[512,4864]{1,0:T(8,128)(2,1)}, bf16[512,4864]{1,0:T(8,128)(2,1)}, bf16[512,4864]{1,0:T(8,128)(2,1)}) fusion(f32[512,9728]{1,0:T(8,128)} %fusion.52, bf16[512,896]{1,0:T(8,128)(2,1)S(1)} %copy-done.22, bf16[4864,896]{1,0:T(8,128)(2,1)} %reshape.350), kind=kOutput, calls=%fused_computation.16 | convolution fusion | flops 4500094976 | bytes 44498944 | tf_op jit(solution)/shard_map/dot_general | solution.py:63
  405.7 15.6 %multiply_reduce_fusion = (f32[896]{0:T(1024)S(1)}, f32[512]{0:T(512)S(1)}, f32[512,896]{1,0:T(8,128)S(1)}) fusion(f32[512,896]{1,0:T(8,128)S(1)} %get-tuple-element.112, f32[512]{0:T(512)S(1)} %add_rsqrt_fusion, f32[896]{0:T(1024)S(1)} %get-tuple-element.107, bf16[896,9728]{1,0:T(8,128)(2,1)} %reshape.349, bf16[512,4864]{1,0:T(8,128)(2,1)} %get-tuple-element.81, ...), kind=kOutput, calls=%fused_computation.46 | convolution fusion | flops 8948152320 | bytes 31075328 | tf_op jit(solution)/shard_map/dot_general | solution.py:63
  427.2 13.0 fusion.28
  440.1 18.4 %fusion = (f32[2,7,512]{2,1,0:T(8,128)S(1)}, f32[2,1024,512,7]{2,1,3,0:T(8,128)}) fusion(f32[2,7,512,1024]{2,3,1,0:T(8,128)} %get-tuple-element.110, f32[2,7,512]{2,1,0:T(8,128)S(1)} %log_add_fusion, bf16[1024,2,64,1]{0,2,3,1:T(8,128)(2,1)S(1)} %bitcast.109, bf16[512,2,7,64]{0,3,2,1:T(8,128)(2,1)S(1)} %bitcast.100), kind=kOutput, calls=%fused_computation.2 | convolution fusion | flops 961537024 | bytes 59957248 | tf_op jit(solution)/shard_map/while/body/eval_jaxpr/qkgd,jkd->kgqj/dot_general | solution.py:209
  458.6 25.2 %fusion.2 = bf16[2,7,512,1024]{2,3,1,0:T(8,128)(2,1)} fusion(f32[2,1024,512,7]{2,1,3,0:T(8,128)} %get-tuple-element.115, f32[2,7,512,1024]{2,3,1,0:T(8,128)} %get-tuple-element.110, f32[2,7,512]{2,1,0:T(8,128)S(1)} %get-tuple-element.114, f32[2,7,512]{2,1,0:T(8,128)S(1)} %log_add_fusion), kind=kLoop, calls=%fused_computation.4 | loop fusion | flops 29360128 | bytes 73457664 | tf_op jit(solution)/shard_map/while/body/eval_jaxpr/convert_element_type | solution.py:213
  483.8 9.7 fusion.32
  493.5 9.2 convolution_multiply_fusion
  505.6 19.2 %fusion.10 = f32[896,9728]{1,0:T(8,128)} fusion(bf16[512,4864]{1,0:T(8,128)(2,1)} %get-tuple-element.81, bf16[512,4864]{1,0:T(8,128)(2,1)} %get-tuple-element.80, f32[512,896]{1,0:T(8,128)} %copy-done.3, f32[896]{0:T(1024)S(1)} %get-tuple-element.107, f32[512]{0:T(512)S(1)} %add_rsqrt_fusion), kind=kOutput, calls=%fused_computation.20 | convolution fusion | flops 8946778112 | bytes 46667264 | tf_op jit(solution)/shard_map/dot_general | solution.py:57
  531.4 11.4 fusion.55
  549.3 45.0 %reshape.363 = f32[32,272384]{1,0:T(8,128)} reshape(f32[896,9728]{1,0:T(8,128)} %fusion.10) | data formatting | bytes 69730304 | tf_op jit(solution)/shard_map/reshape | solution.py:194
  594.3 19.9 %reshape.365 = f32[32,136192]{1,0:T(8,128)} reshape(f32[4864,896]{1,0:T(8,128)} %fusion.55) | data formatting | bytes 34865152 | tf_op jit(solution)/shard_map/reshape | solution.py:195
  616.4 3.6 fusion.36
  620.0 4.1 reshape.357
  624.2 11.2 add_convert_fusion
  640.1 44.1 %all-reduce.8 = (f32[32,56]{1,0:T(8,128)S(1)}, f32[32,36]{1,0:T(8,128)S(1)}) all-reduce(f32[32,56]{1,0:T(8,128)S(1)} %pad_maximum_fusion.6, f32[32,36]{1,0:T(8,128)S(1)} %reshape.359), channel_id=2, replica_groups=mesh['fsdp'=32] {'fsdp'}, use_global_device_ids=true, to_apply=%region_13.14.clone | all-reduce | flops 2944 | bytes 23552
  688.5 783.1 %all-reduce.13.cloned.1.call-done = (f32[32,32256]{1,0:T(8,128)}, f32[32,25088]{1,0:T(8,128)}, f32[32,272384]{1,0:T(8,128)}, f32[32,136192]{1,0:T(8,128)}) async-done(((f32[32,32256]{1,0:T(8,128)}, f32[32,25088]{1,0:T(8,128)}, f32[32,272384]{1,0:T(8,128)}, f32[32,136192]{1,0:T(8,128)}), (f32[32,32256]{1,0:T(8,128)}, f32[32,25088]{1,0:T(8,128)}, f32[32,272384]{1,0:T(8,128)}, ...) | async-done | bytes 59637776
  1475.9 5.3 constant_dynamic-slice_fusion.1
  (153 shorter events, 72.0 us)
Async XLA Ops:
  7.2 51.7 %copy-start.4 = (bf16[512,896]{1,0:T(8,128)(2,1)S(1)}, bf16[512,896]{1,0:T(8,128)(2,1)}, u32[]{:S(2)}) copy-start(bf16[512,896]{1,0:T(8,128)(2,1)} %param.9) | copy-start | bytes 2752516
  7.2 66.2 %all-gather.13.cloned.1.call-start = ((), (), s32[]{:S(2)}) async-start(), calls=%async_computation.3 | async-start | bytes 3311616 | tf_op jit(solution)/shard_map/all_gather | solution.py:108
  8.8 128.7 %all-gather.11.cloned.1.call-start = ((), (), s32[]{:S(2)}) async-start(), calls=%async_computation.2 | async-start | bytes 4257792 | tf_op jit(solution)/shard_map/all_gather | solution.py:106
  10.5 208.8 %all-gather.9.cloned.1.call-start = ((), (), s32[]{:S(2)}) async-start(), calls=%async_computation.1 | async-start | bytes 8988672 | tf_op jit(solution)/shard_map/all_gather | solution.py:112
  11.2 327.4 %all-gather.7.cloned.1.call-start = ((), (), s32[]{:S(2)}) async-start(), calls=%async_computation | async-start | bytes 17977344 | tf_op jit(solution)/shard_map/all_gather | solution.py:111
  11.8 1459.9 %all-reduce.13.cloned.1.call-start = ((), (), s32[]{:S(2)}) async-start(), calls=%async_computation.4 | async-start | bytes 119275520
  57.9 111.8 %copy-start.9 = (f32[512,64]{0,1:T(8,128)}, f32[512,64]{0,1:T(8,128)S(1)}, u32[]{:S(2)}) copy-start(f32[512,64]{0,1:T(8,128)S(1)} %get-tuple-element.105) | copy-start | bytes 393220
  57.9 111.8 %copy-start.11 = (f32[512,64]{0,1:T(8,128)}, f32[512,64]{0,1:T(8,128)S(1)}, u32[]{:S(2)}) copy-start(f32[512,64]{0,1:T(8,128)S(1)} %get-tuple-element.106) | copy-start | bytes 393220
  59.1 94.8 %copy-start.29 = (f32[512]{0:T(512)}, f32[512]{0:T(512)S(1)}, u32[]{:S(2)}) copy-start(f32[512]{0:T(512)S(1)} %add_rsqrt_fusion.1) | copy-start | bytes 6148
  59.2 94.8 %copy-start.27 = (f32[896]{0:T(1024)}, f32[896]{0:T(1024)S(1)}, u32[]{:S(2)}) copy-start(f32[896]{0:T(1024)S(1)} %get-tuple-element.108) | copy-start | bytes 10756
  159.4 5.2 copy-start.21
  159.4 12.1 collective-permute-start
  166.3 6.4 collective-permute-start.1
  170.3 15.7 %copy-start = (bf16[512,2,7,64]{0,3,2,1:T(8,128)(2,1)}, bf16[512,2,7,64]{0,3,2,1:T(8,128)(2,1)S(1)}, u32[]{:S(2)}) copy-start(bf16[512,2,7,64]{0,3,2,1:T(8,128)(2,1)S(1)} %fusion.24) | copy-start | bytes 2752516
  171.5 14.6 copy-start.17
  173.7 12.3 copy-start.19
  198.7 12.6 copy-start.5
  198.7 12.6 copy-start.15
  212.7 193.0 %copy-start.3 = (f32[512,896]{1,0:T(8,128)}, f32[512,896]{1,0:T(8,128)S(1)}, u32[]{:S(2)}) copy-start(f32[512,896]{1,0:T(8,128)S(1)} %get-tuple-element.112) | copy-start | bytes 5505028
  368.5 18.3 %copy-start.22 = (bf16[512,896]{1,0:T(8,128)(2,1)S(1)}, bf16[512,896]{1,0:T(8,128)(2,1)}, u32[]{:S(2)}) copy-start(bf16[512,896]{1,0:T(8,128)(2,1)} %param.17) | copy-start | bytes 2752516
  405.7 15.7 %copy-start.23 = (bf16[512,896]{1,0:T(8,128)(2,1)S(1)}, bf16[512,896]{1,0:T(8,128)(2,1)}, u32[]{:S(2)}) copy-start(bf16[512,896]{1,0:T(8,128)(2,1)} %param.17) | copy-start | bytes 2752516
  458.6 25.2 %copy-start.1 = (bf16[512,2,7,64]{0,3,2,1:T(8,128)(2,1)S(1)}, bf16[512,2,7,64]{0,3,2,1:T(8,128)(2,1)}, u32[]{:S(2)}) copy-start(bf16[512,2,7,64]{0,3,2,1:T(8,128)(2,1)} %copy-done) | copy-start | bytes 2752516
  483.8 9.7 copy-start.18
  483.8 9.7 copy-start.20
  493.5 9.2 copy-start.26
  524.8 6.6 copy-start.24
  526.5 88.9 %collective-permute-start.3 = (bf16[512,2,64]{0,2,1:T(8,128)(2,1)}, bf16[512,2,64]{0,2,1:T(8,128)(2,1)}, u32[]{:S(2)}, u32[]{:S(2)}) collective-permute-start(bf16[512,2,64]{0,2,1:T(8,128)(2,1)} %slice.122), channel_id=1, source_target_pairs={{1,0},{2,1},{3,2},{4,3},{5,4},{6,5},{7,6},{8,7},{9,8},{10,9},{11,1... | collective-permute-start | bytes 393224 | tf_op jit(solution)/shard_map/ppermute | solution.py:23
  528.4 85.7 %collective-permute-start.2 = (bf16[512,2,64]{0,2,1:T(8,128)(2,1)}, bf16[512,2,64]{0,2,1:T(8,128)(2,1)}, u32[]{:S(2)}, u32[]{:S(2)}) collective-permute-start(bf16[512,2,64]{0,2,1:T(8,128)(2,1)} %slice.123), channel_id=1, source_target_pairs={{1,0},{2,1},{3,2},{4,3},{5,4},{6,5},{7,6},{8,7},{9,8},{10,9},{11,1... | collective-permute-start | bytes 393224 | tf_op jit(solution)/shard_map/ppermute | solution.py:23
  531.4 11.5 copy-start.12
  614.1 2.3 copy-start.30
  624.2 11.2 copy-start.8
  624.2 11.2 copy-start.14
  (9 other events, 17.3 us)
Sparse Core Ops, SparseCore 0:
  11.5 61.8 all-gather.12
  76.9 60.6 all-gather.10
  140.5 78.6 all-gather.8
  221.9 116.6 all-gather.6
  624.2 847.3 all-reduce.12
where the time goes:
time: 1500 us; the launch traced here: 1490 us
  waiting for transfers between devices  957 us (64%)
  matrix products  186 us (12%)
  local copies, waits for them, and re-layouts  159 us (11%)
  blocking collectives  86.4 us (6%)
  other arithmetic  79.4 us (5%)
    unnamed x6, waiting for transfers between devices  784 us
    all_gather x1, waiting for transfers between devices, local(): lax.all_gather(w_gate_up, 'fsdp', axis=0, tiled=True)  103 us
    unnamed x2, blocking collectives  86.4 us
    all_gather x1, waiting for transfers between devices, local(): lax.all_gather(w_qkv, 'fsdp', axis=0, tiled=True)  49.8 us
    reshape x2, local copies, waits for them, and re-layouts, unpack_mlp(): return (gu_flat.reshape(width, 2 * FF), down_flat.reshape(FF, width))  46.3 us
    reshape x1, local copies, waits for them, and re-layouts, local(): grad_wgu.reshape(n_devices, -1)  45 us
    dot_general x4, matrix products, back_dot(): lax.dot_general(left, right, (((1,), (1,)), ((), ())), preferred_element_...  39.8 us
    dot_general x4, matrix products, outer_sum(): lax.dot_general(left, right, (((0,), (0,)), ((), ())), preferred_element_...  37 us
  transfers between devices with their start and end apart: 9, of which 5 were waited for; matrix products, arithmetic and copies ran while one was open for 14% of the time, Pallas kernels for 0%

commit v1 on v0

--- a/solution.py
+++ b/solution.py
@@ -79,6 +79,33 @@
 def unpack_mlp(params, width):
     gu_flat, down_flat = params
     return (gu_flat.reshape(width, 2 * FF), down_flat.reshape(FF, width))
+
+
+def partner_swap(x, bit):
+    peers = lax.axis_size("fsdp")
+    return lax.ppermute(x, "fsdp", [(i, i ^ (1 << bit)) for i in range(peers)])
+
+
+def my_bit(bit):
+    return (lax.axis_index("fsdp") >> bit) & 1
+
+
+def halve(x, axis, bit):
+    mine = my_bit(bit)
+    sent = lax.dynamic_index_in_dim(x, 1 - mine, axis, keepdims=False).astype(jnp.bfloat16)
+    kept = lax.dynamic_index_in_dim(x, mine, axis, keepdims=False)
+    return kept.astype(jnp.float32) + partner_swap(sent, bit).astype(jnp.float32)
+
+
+def reduce_to_owner(x, bits, order):
+    left = list(bits)
+    x = x.reshape((2,) * len(left) + x.shape[1:])
+    for bit in order:
+        x = halve(x, left.index(bit), bit)
+        left.remove(bit)
+        if left:
+            x = x.astype(jnp.bfloat16)
+    return x
 
 
 def norm_back(grad_normed, hidden, factor, gain):
@@ -101,18 +128,41 @@
     scale = 1.0 / math.sqrt(HD)
     block_rows = min(tok_rows, 512)
     block_count = tok_rows // block_rows
-    attn_params = (
-        lax.all_gather(gains, "fsdp", axis=0, tiled=True),
-        lax.all_gather(w_qkv, "fsdp", axis=0, tiled=True),
-        lax.all_gather(b_qkv, "fsdp", axis=0, tiled=True),
-        lax.all_gather(w_out, "fsdp", axis=0, tiled=True),
-    )
-    mlp_params = (
-        lax.all_gather(w_gate_up, "fsdp", axis=0, tiled=True),
-        lax.all_gather(w_down, "fsdp", axis=0, tiled=True),
-    )
-    gain_one, gain_two, wqkv, bias, wout = unpack_attention(attn_params, width)
-    wgu, wdown = unpack_mlp(mlp_params, width)
+    rows_own = width // n_devices
+    core = my_bit(0)
+    chips = n_devices // 2
+    attn_sizes = (w_qkv.shape[0], w_out.shape[0], gains.shape[0], b_qkv.shape[0])
+    attn_flat = jnp.concatenate([w_qkv, w_out, gains, b_qkv])
+    attn_flat = jnp.pad(attn_flat, (0, -attn_flat.shape[0] % 1024))
+    attn_all = lax.all_gather(attn_flat, "fsdp", axis=0, tiled=True).reshape(n_devices, -1)
+    pieces, at = [], 0
+    for size in attn_sizes:
+        pieces.append(attn_all[:, at : at + size].reshape(-1))
+        at += size
+    gain_one, gain_two, wqkv, bias, wout = unpack_attention(
+        (pieces[2], pieces[0], pieces[3], pieces[1]), width
+    )
+    whole_rows = width % n_devices == 0
+    if whole_rows:
+        gu_own = w_gate_up.reshape(rows_own, 2, FF)
+        gu_own = (gu_own[:, 0], gu_own[:, 1])
+        gu_kept = jnp.where(core == 0, gu_own[0], gu_own[1])
+        gu_came = partner_swap(jnp.where(core == 0, gu_own[1], gu_own[0]), 0)
+        gu_chip = jnp.where(
+            core == 0,
+            jnp.concatenate([gu_kept, gu_came]),
+            jnp.concatenate([gu_came, gu_kept]),
+        )
+        gu_chip, attn_all = lax.optimization_barrier((gu_chip, attn_all))
+        gu_all = lax.all_gather(gu_chip, "fsdp", axis=0, tiled=True)
+        gu_all = gu_all.reshape(chips, 2, 2 * rows_own, FF)
+        wgate = gu_all[:, 0].reshape(width, FF)
+        wup = gu_all[:, 1].reshape(width, FF)
+    else:
+        gu_all = lax.all_gather(w_gate_up, "fsdp", axis=0, tiled=True).reshape(width, 2 * FF)
+        wgate, wup = gu_all[:, :FF], gu_all[:, FF:]
+    down_own, gu_all = lax.optimization_barrier((w_down.reshape(FF // n_devices, width), gu_all))
+    wdown = lax.all_gather(down_own, "fsdp", axis=0, tiled=True)
     base_index = lax.axis_index("fsdp") * tok_rows
     token_index, segment, position = segment_info(lengths, base_index, tok_rows)
     prev_index, prev_segment, unused_pos = segment_info(lengths, base_index - tok_rows, tok_rows)
@@ -163,43 +213,55 @@
     middle = hidden + jnp.dot(attended, wout, preferred_element_type=jnp.float32)
     factor_two = lax.rsqrt(jnp.mean(middle * middle, axis=1, keepdims=True) + EPSILON)
     normed_two = (middle * factor_two * gain_two).astype(jnp.bfloat16)
-    gate_up = jnp.dot(normed_two, wgu, preferred_element_type=jnp.float32)
-    gate_pre = gate_up[:, :FF]
-    up_pre = gate_up[:, FF:]
+    gate_pre = jnp.dot(normed_two, wgate, preferred_element_type=jnp.float32)
+    up_pre = jnp.dot(normed_two, wup, preferred_element_type=jnp.float32)
     sigma = jax.nn.sigmoid(gate_pre)
     silu_gate = gate_pre * sigma
     product = (silu_gate * up_pre).astype(jnp.bfloat16)
     output = (middle + jnp.dot(product, wdown, preferred_element_type=jnp.float32)).astype(
         jnp.bfloat16
     )
-    back_mlp = (
-        lax.all_gather(w_gate_up, "fsdp", axis=0, tiled=True),
-        lax.all_gather(w_down, "fsdp", axis=0, tiled=True),
-    )
-    back_attn = (
-        lax.all_gather(gains, "fsdp", axis=0, tiled=True),
-        lax.all_gather(w_qkv, "fsdp", axis=0, tiled=True),
-        lax.all_gather(b_qkv, "fsdp", axis=0, tiled=True),
-        lax.all_gather(w_out, "fsdp", axis=0, tiled=True),
-    )
-    gain_one_b, gain_two_b, wqkv_b, unused_bias, wout_b = unpack_attention(back_attn, width)
-    wgu_b, wdown_b = unpack_mlp(back_mlp, width)
-    grad_down = outer_sum(product, grad_out)
-    grad_product = back_dot(grad_out, wdown_b)
+    bits = tuple(range(n_devices.bit_length() - 2, -1, -1))
+    far = bits[: len(bits) - 4]
+    grad_down = outer_sum(product, grad_out).astype(jnp.bfloat16)
+    down_parts = halve(grad_down.reshape(chips, 2, -1, width), 1, 0).astype(jnp.bfloat16)
+    down_sum = reduce_to_owner(down_parts, bits[:-1], (3, 1, 2) + far)
+    grad_product = back_dot(grad_out, wdown)
     grad_gate = grad_product * up_pre * sigma * (1.0 + gate_pre * (1.0 - sigma))
     grad_up = grad_product * silu_gate
-    grad_gu = jnp.concatenate([grad_gate, grad_up], axis=1).astype(jnp.bfloat16)
-    grad_wgu = outer_sum(normed_two, grad_gu)
-    mlp_grads = (
-        lax.psum_scatter(grad_wgu.reshape(n_devices, -1), "fsdp", scatter_dimension=0, tiled=True),
-        lax.psum_scatter(grad_down.reshape(n_devices, -1), "fsdp", scatter_dimension=0, tiled=True),
-    )
-    grad_normed_two = back_dot(grad_gu, wgu_b)
-    grad_middle_norm, grad_gain_two = norm_back(grad_normed_two, middle, factor_two, gain_two_b)
+    grad_gate = grad_gate.astype(jnp.bfloat16)
+    grad_up = grad_up.astype(jnp.bfloat16)
+    if whole_rows:
+        gu_sent = outer_sum(normed_two, jnp.where(core == 0, grad_up, grad_gate))
+        gu_came = partner_swap(gu_sent.astype(jnp.bfloat16), 0)
+        gu_kept = outer_sum(normed_two, jnp.where(core == 0, grad_gate, grad_up))
+        gu_parts = (gu_kept + gu_came.astype(jnp.float32)).astype(jnp.bfloat16)
+        gu_parts = gu_parts.reshape(chips, 2 * rows_own, FF)
+        gu_sums = (
+            reduce_to_owner(gu_parts[:, :, : FF // 2], bits[:-1], (1, 2, 3) + far),
+            reduce_to_owner(gu_parts[:, :, FF // 2 :], bits[:-1], (2, 3, 1) + far),
+        )
+        gu_sum = jnp.concatenate(gu_sums, axis=1).reshape(2, rows_own, FF)
+        gu_kept = lax.dynamic_index_in_dim(gu_sum, core, 0, keepdims=False)
+        gu_came = partner_swap(lax.dynamic_index_in_dim(gu_sum, 1 - core, 0, keepdims=False), 0)
+        grad_wgu = jnp.concatenate(
+            [jnp.where(core == 0, gu_kept, gu_came), jnp.where(core == 0, gu_came, gu_kept)], axis=1
+        )
+    else:
+        grad_gu = jnp.concatenate([grad_gate, grad_up], axis=1)
+        gu_parts = outer_sum(normed_two, grad_gu).astype(jnp.bfloat16)
+        grad_wgu = reduce_to_owner(gu_parts.reshape(n_devices, -1), bits, (0, 1, 2, 3) + far)
+    grad_normed_two = back_dot(grad_gate, wgate) + back_dot(grad_up, wup)
+    grad_middle_norm, grad_gain_two = norm_back(grad_normed_two, middle, factor_two, gain_two)
     grad_middle = grad_out.astype(jnp.float32) + grad_middle_norm
     grad_branch = grad_middle.astype(jnp.bfloat16)
-    grad_wout = outer_sum(attended, grad_branch)
-    grad_att = back_dot(grad_branch, wout_b).astype(jnp.bfloat16)
+    grad_wout = outer_sum(attended, grad_branch).astype(jnp.bfloat16)
+    wout_sum = reduce_to_owner(
+        grad_wout.reshape((n_devices, -1, width) if whole_rows else (n_devices, -1)),
+        bits,
+        (0, 2, 3, 1) + far,
+    )
+    grad_att = back_dot(grad_branch, wout).astype(jnp.bfloat16)
     grad_att_four = grad_att.reshape(tok_rows, KV_HEADS, groups, HD)
 
     def back_block(number, carried):
@@ -251,31 +313,32 @@
     )
     grad_wqkv = outer_sum(normed_one, grad_linear)
     grad_bias = jnp.sum(grad_linear.astype(jnp.float32), axis=0)
-    grad_normed_one = back_dot(grad_linear, wqkv_b)
-    grad_hidden_norm, grad_gain_one = norm_back(grad_normed_one, hidden, factor_one, gain_one_b)
+    grad_normed_one = back_dot(grad_linear, wqkv)
+    grad_hidden_norm, grad_gain_one = norm_back(grad_normed_one, hidden, factor_one, gain_one)
     grad_tokens = grad_middle + grad_hidden_norm
-    bias_full = b_qkv.shape[0] * n_devices
-    grad_bias_full = jnp.concatenate([grad_bias, jnp.zeros((bias_full - QKV,), jnp.float32)])
+    gains_own, bias_own = gains.shape[0], b_qkv.shape[0]
+    grad_bias_full = jnp.pad(grad_bias, (0, bias_own * n_devices - QKV))
     grad_gains_full = jnp.concatenate([grad_gain_one, grad_gain_two])
-    attn_grads = (
-        lax.psum_scatter(
-            grad_gains_full.reshape(n_devices, -1), "fsdp", scatter_dimension=0, tiled=True
-        ),
-        lax.psum_scatter(grad_wqkv.reshape(n_devices, -1), "fsdp", scatter_dimension=0, tiled=True),
-        lax.psum_scatter(
-            grad_bias_full.reshape(n_devices, -1), "fsdp", scatter_dimension=0, tiled=True
-        ),
-        lax.psum_scatter(grad_wout.reshape(n_devices, -1), "fsdp", scatter_dimension=0, tiled=True),
-    )
+    vectors = jnp.concatenate(
+        [grad_gains_full.reshape(n_devices, -1), grad_bias_full.reshape(n_devices, -1)], axis=1
+    )
+    if whole_rows:
+        vectors = jnp.pad(vectors, ((0, 0), (0, QKV - vectors.shape[1])))[:, None]
+        grad_wqkv = grad_wqkv.reshape(n_devices, rows_own, QKV)
+    else:
+        grad_wqkv = grad_wqkv.reshape(n_devices, -1)
+    last = jnp.concatenate([grad_wqkv, vectors], axis=1).astype(jnp.bfloat16)
+    last_sum = reduce_to_owner(last, bits, (0, 1, 2, 3) + far).reshape(-1)
+    qkv_own = w_qkv.shape[0]
     return (
         output,
         grad_tokens,
-        attn_grads[0].reshape(-1),
-        attn_grads[1].reshape(-1),
-        attn_grads[2].reshape(-1),
-        attn_grads[3].reshape(-1),
-        mlp_grads[0].reshape(-1),
-        mlp_grads[1].reshape(-1),
+        last_sum[qkv_own : qkv_own + gains_own],
+        last_sum[:qkv_own],
+        last_sum[qkv_own + gains_own : qkv_own + gains_own + bias_own],
+        wout_sum.reshape(-1),
+        grad_wgu.reshape(-1),
+        down_sum.reshape(-1),
     )
 
 

time: 1500 us -> 711 us (0.47)
  waiting for transfers between devices: 957 us -> 324 us
  local copies, waits for them, and re-layouts: 159 us -> 66.9 us
  blocking collectives: 86.4 us -> 0 us
  starting transfers between devices: 9 us -> 45.7 us
    unnamed x6 -> x3, waiting for transfers between devices: 784 us -> 0.05 us
    ppermute x0 -> x26, waiting for transfers between devices: none -> 146 us  [partner_swap(): return lax.ppermute(x, 'fsdp', [(i, i ^ 1 << bit) for i in range(peers)])]
    reshape x12 -> x8, local copies, waits for them, and re-layouts: 132 us -> 10.6 us  [the longest x1 5.17 us: local(): lax.all_gather(attn_flat, 'fsdp', axis=0, tiled=True).reshape(n_devices, -1)]
    unnamed x2 -> x0, blocking collectives: 86.4 us -> none
    ppermute x0 -> x26, starting transfers between devices: none -> 36.3 us  [partner_swap(): return lax.ppermute(x, 'fsdp', [(i, i ^ 1 << bit) for i in range(peers)])]
    all_gather x2 -> x0, other arithmetic: 23 us -> none  [the longest x1 12.2 us: local(): lax.all_gather(w_qkv, 'fsdp', axis=0, tiled=True)]
    dot_general x4 -> x5, matrix products: 37 us -> 33.7 us  [outer_sum(): lax.dot_general(left, right, (((0,), (0,)), ((), ())), preferred_element_...]
    dot_general x4 -> x5, matrix products: 39.8 us -> 41.9 us  [back_dot(): lax.dot_general(left, right, (((1,), (1,)), ((), ())), preferred_element_...]
  transfers between devices with their start and end apart: 9 -> 33, of which waited for: 5 -> 16; matrix products, arithmetic and copies ran while one was open for 14% -> 25% of each run, Pallas kernels for 0% -> 0%
where the time goes in v1:
time: 711 us; the launch traced here: 703 us
  waiting for transfers between devices  324 us (46%)
  matrix products  185 us (26%)
  local copies, waits for them, and re-layouts  66.9 us (9%)
  other arithmetic  65.6 us (9%)
  starting transfers between devices  45.7 us (6%)
  between operations  15.4 us (2%)
    ppermute x26, waiting for transfers between devices, partner_swap(): return lax.ppermute(x, 'fsdp', [(i, i ^ 1 << bit) for i in range(peers)])  146 us
    all_gather x1, waiting for transfers between devices, local(): gu_all = lax.all_gather(gu_chip, 'fsdp', axis=0, tiled=True)  116 us
    all_gather x1, waiting for transfers between devices, local(): lax.all_gather(attn_flat, 'fsdp', axis=0, tiled=True).reshape(n_devices, -1)  57.9 us
    dot_general x5, matrix products, back_dot(): lax.dot_general(left, right, (((1,), (1,)), ((), ())), preferred_element_...  41.9 us
    ppermute x26, starting transfers between devices, partner_swap(): return lax.ppermute(x, 'fsdp', [(i, i ^ 1 << bit) for i in range(peers)])  36.3 us
    dot_general x5, matrix products, outer_sum(): lax.dot_general(left, right, (((0,), (0,)), ((), ())), preferred_element_...  33.7 us
    convert_element_type x1, other arithmetic, back_block(): grad_scores = (probs * (grad_probs - inner)).astype(jnp.bfloat16)  25.1 us
    dot_general x1, matrix products, back_block(): jnp.einsum('qkgd,jkd->kgqj', grad_att_four, value_block, preferred_elemen...  18.7 us
  transfers between devices with their start and end apart: 33, of which 16 were waited for; matrix products, arithmetic and copies ran while one was open for 25% of the time, Pallas kernels for 0%

profile of v1, /device:TPU:0, one launch (start us, length us, event | category | flops | bytes accessed | tf_op | source)
XLA Modules:
  0.0 702.8 jit_solution(16752354043904735620)
XLA Ops:
  16.9 57.9 %all-gather.4.cloned.1.call-done = bf16[1867776]{0:T(1024)(128)(2,1)} async-done(((bf16[58368]{0:T(1024)(128)(2,1)}), bf16[1867776]{0:T(1024)(128)(2,1)}) %all-gather.4.cloned.1.call-update) | async-done | bytes 3735568 | tf_op jit(solution)/shard_map/all_gather | solution.py:137
  74.8 5.2 reshape.421
  81.1 116.0 %all-gather.6.cloned.1.call-done = bf16[1792,4864]{1,0:T(8,128)(2,1)} async-done(((bf16[56,4864]{1,0:T(8,128)(2,1)}), bf16[1792,4864]{1,0:T(8,128)(2,1)}) %all-gather.6.cloned.1.call-update) | async-done | bytes 17432592 | tf_op jit(solution)/shard_map/all_gather | solution.py:157
  203.1 4.2 reshape_reshape.9
  231.3 11.9 %fusion.85 = (f32[2,7,512]{2,1,0:T(8,128)S(1)}, f32[2,7,512,1024]{2,3,1,0:T(8,128)}) fusion(bf16[512,2,7,64]{0,3,2,1:T(8,128)(2,1)S(1)} %fusion.41, bf16[512,2,64]{0,2,1:T(8,128)(2,1)S(1)} %bitcast.281, bf16[512,2,64]{0,2,1:T(8,128)(2,1)S(1)} %bitcast.283, pred[512,1024]{0,1:T(8,128)(4,1)S(1)} %and_and_fusion), kind=kOutput, calls=%fused_computation.212 | convolution fusion | flops 962061312 | bytes 31092736 | tf_op jit(solution)/shard_map/while/body/eval_jaxpr/qkgd,jkd->kgqj/dot_general | solution.py:196
  243.3 12.6 %fusion.3 = f32[2,7,512]{2,1,0:T(8,128)S(1)} fusion(f32[2,7,512,1024]{2,3,1,0:T(8,128)} %get-tuple-element.116, f32[2,7,512]{2,1,0:T(8,128)S(1)} %get-tuple-element.115), kind=kLoop, calls=%fused_computation.9 | loop fusion | flops 14672896 | bytes 29417472 | tf_op jit(solution)/shard_map/while/body/eval_jaxpr/reduce_sum | solution.py:206
  255.9 13.4 %fusion.45 = bf16[2,64,7,512]{3,1,2,0:T(8,128)(2,1)} fusion(bf16[1024,2,64,1]{0,2,3,1:T(8,128)(2,1)S(1)} %bitcast.286, f32[2,7,512,1024]{2,3,1,0:T(8,128)} %get-tuple-element.116, f32[2,7,512]{2,1,0:T(8,128)S(1)} %fusion.3, f32[2,7,512]{2,1,0:T(8,128)} %copy-done.43), kind=kOutput, calls=%fused_computation.92 | convolution fusion | flops 962002944 | bytes 30597120 | tf_op jit(solution)/shard_map/while/body/eval_jaxpr/kgqj,jkd->qkgd/dot_general | solution.py:208
  277.2 9.9 %fusion.87 = f32[512,4864]{1,0:T(8,128)} fusion(bf16[512,896]{1,0:T(8,128)(2,1)} %multiply_convert_fusion.1, bf16[896,4864]{1,0:T(8,128)(2,1)S(1)} %bitcast.268), kind=kOutput, calls=%fused_computation.214 | convolution fusion | flops 4462739456 | bytes 19595264 | tf_op jit(solution)/shard_map/dot_general | solution.py:217
  287.2 8.2 %fusion.86 = f32[512,4864]{1,0:T(8,128)} fusion(bf16[512,896]{1,0:T(8,128)(2,1)S(1)} %copy-done.18, bf16[896,4864]{1,0:T(8,128)(2,1)S(1)} %bitcast.270), kind=kOutput, calls=%fused_computation.213 | convolution fusion | flops 4462739456 | bytes 19595264 | tf_op jit(solution)/shard_map/dot_general | solution.py:216
  295.4 16.8 %fusion.12 = (bf16[512,4864]{1,0:T(8,128)(2,1)S(1)}, bf16[512,4864]{1,0:T(8,128)(2,1)}, bf16[512,4864]{1,0:T(8,128)(2,1)}) fusion(f32[512,4864]{1,0:T(8,128)} %fusion.86, f32[512,4864]{1,0:T(8,128)} %fusion.87, bf16[4864,896]{1,0:T(8,128)(2,1)} %all-gather.8.cloned.1.call-done, bf16[512,896]{1,0:T(8,128)(2,1)} %param.17), kind=kOutput, calls=%fused_computation.20 | convolution fusion | flops 4500094976 | bytes 44498944 | tf_op jit(solution)/shard_map/dot_general | solution.py:63
  312.2 12.7 %fusion.88 = f32[512,896]{1,0:T(8,128)} fusion(bf16[512,4864]{1,0:T(8,128)(2,1)} %get-tuple-element.77, bf16[896,4864]{1,0:T(8,128)(2,1)} %bitcast.271), kind=kOutput, calls=%fused_computation.215 | convolution fusion | flops 4462739456 | bytes 15532032 | tf_op jit(solution)/shard_map/dot_general | solution.py:63
  324.9 7.3 %multiply_reduce_fusion = (bf16[896]{0:T(1024)(128)(2,1)S(1)}, f32[512]{0:T(512)S(1)}, f32[512,896]{1,0:T(8,128)S(1)}) fusion(f32[512,896]{1,0:T(8,128)S(1)} %copy-done.11, f32[512]{0:T(512)S(1)} %add_rsqrt_fusion, f32[896]{0:T(1024)S(1)} %reshape.449, f32[512,896]{1,0:T(8,128)} %fusion.88, bf16[512,4864]{1,0:T(8,128)(2,1)S(1)} %get-tuple-element.76, ...), kind=kOutput, calls=%fused_computation.82 | convolution fusion | flops 4465949184 | bytes 19211520 | tf_op jit(solution)/shard_map/dot_general | solution.py:63
  338.0 7.3 %convolution_convert_fusion.1 = bf16[896,4864]{1,0:T(8,128)(2,1)} fusion(bf16[512,896]{1,0:T(8,128)(2,1)S(1)} %copy-done.19, bf16[512,4864]{1,0:T(8,128)(2,1)S(1)} %get-tuple-element.76, bf16[512,4864]{1,0:T(8,128)(2,1)S(1)} %bitcast.275, pred[]{:T(512)S(6)} %eq.50), kind=kOutput, calls=%fused_computation.25 | convolution fusion | flops 4469587968 | bytes 19595264 | tf_op jit(solution)/shard_map/dot_general | solution.py:57
  346.8 11.8 %fusion.46 = f32[1024,2,64]{0,2,1:T(8,128)S(1)} fusion(bf16[512,2,7,64]{0,3,2,1:T(8,128)(2,1)S(1)} %bitcast.272, f32[2,7,512,1024]{2,3,1,0:T(8,128)} %get-tuple-element.116, f32[2,7,512]{2,1,0:T(8,128)S(1)} %log_add_fusion), kind=kOutput, calls=%fused_computation.94 | convolution fusion | flops 954204160 | bytes 30830592 | tf_op jit(solution)/shard_map/while/body/eval_jaxpr/kgqj,qkgd->jkd/dot_general | solution.py:284
  358.7 18.7 %fusion = (f32[2,7,512]{2,1,0:T(8,128)S(1)}, f32[2,1024,512,7]{2,1,3,0:T(8,128)}) fusion(f32[2,7,512,1024]{2,3,1,0:T(8,128)} %get-tuple-element.116, f32[2,7,512]{2,1,0:T(8,128)S(1)} %log_add_fusion, bf16[1024,2,64,1]{0,2,3,1:T(8,128)(2,1)S(1)} %bitcast.287, bf16[512,2,7,64]{0,3,2,1:T(8,128)(2,1)S(1)} %bitcast.273), kind=kOutput, calls=%fused_computation.2 | convolution fusion | flops 961537024 | bytes 59957248 | tf_op jit(solution)/shard_map/while/body/eval_jaxpr/qkgd,jkd->kgqj/dot_general | solution.py:271
  377.4 25.1 %fusion.2 = bf16[2,7,512,1024]{2,3,1,0:T(8,128)(2,1)} fusion(f32[2,1024,512,7]{2,1,3,0:T(8,128)} %get-tuple-element.121, f32[2,7,512,1024]{2,3,1,0:T(8,128)} %get-tuple-element.116, f32[2,7,512]{2,1,0:T(8,128)S(1)} %get-tuple-element.120, f32[2,7,512]{2,1,0:T(8,128)S(1)} %log_add_fusion), kind=kLoop, calls=%fused_computation.4 | loop fusion | flops 29360128 | bytes 73457664 | tf_op jit(solution)/shard_map/while/body/eval_jaxpr/convert_element_type | solution.py:275
  402.5 9.7 %fusion.50 = f32[1024,2,64]{0,2,1:T(8,128)S(1)} fusion(bf16[512,2,7,64]{0,3,2,1:T(8,128)(2,1)S(1)} %copy-done.1, bf16[2,7,512,1024]{2,3,1,0:T(8,128)(2,1)} %fusion.2), kind=kOutput, calls=%fused_computation.97 | convolution fusion | flops 939655168 | bytes 16121856 | tf_op jit(solution)/shard_map/while/body/eval_jaxpr/kgqj,qkgd->jkd/dot_general | solution.py:281
  412.3 7.9 %convolution_multiply_fusion = f32[2,64,7,512]{3,1,2,0:T(8,128)S(1)} fusion(bf16[2,7,512,1024]{2,3,1,0:T(8,128)(2,1)} %fusion.2, bf16[512,2,64]{0,2,1:T(8,128)(2,1)S(1)} %bitcast.282, bf16[512,2,64]{0,2,1:T(8,128)(2,1)S(1)} %bitcast.284), kind=kOutput, calls=%fused_computation.89 | convolution fusion | flops 940507136 | bytes 16777216 | tf_op jit(solution)/shard_map/while/body/eval_jaxpr/kgqj,jkd->qkgd/dot_general | solution.py:277
  429.2 8.0 %convolution_convert_fusion = bf16[4864,896]{1,0:T(8,128)(2,1)S(1)} fusion(bf16[512,4864]{1,0:T(8,128)(2,1)} %get-tuple-element.78, bf16[512,896]{1,0:T(8,128)(2,1)S(1)} %copy-done.41), kind=kOutput, calls=%fused_computation.24 | convolution fusion | flops 4467097600 | bytes 14614528 | tf_op jit(solution)/shard_map/dot_general | solution.py:57
  460.5 10.9 %add_convert_fusion.1 = bf16[512,896]{1,0:T(8,128)(2,1)} fusion(f32[512,896]{1,0:T(8,128)S(1)} %copy-done.12, bf16[512,4864]{1,0:T(8,128)(2,1)} %get-tuple-element.78, bf16[4864,896]{1,0:T(8,128)(2,1)} %all-gather.8.cloned.1.call-done), kind=kOutput, calls=%fused_computation.85 | convolution fusion | flops 4463656960 | bytes 16449536 | tf_op jit(solution)/shard_map/dot_general | solution.py:221
  475.1 10.5 %collective-permute-done.11 = bf16[2,2,2,28,896]{4,3,2,1,0:T(8,128)(2,1)S(1)} collective-permute-done((bf16[2,2,2,28,896]{4,3,2,1,0:T(8,128)(2,1)S(1)}, bf16[2,2,2,28,896]{4,3,2,1,0:T(8,128)(2,1)S(1)}, u32[]{:S(2)}, u32[]{:S(2)}) %collective-permute-start.11) | collective-permute-done | bytes 401440 | tf_op jit(solution)/shard_map/ppermute | solution.py:86
  504.8 36.5 %collective-permute-done.14 = bf16[28,896]{1,0:T(8,128)(2,1)S(1)} collective-permute-done((bf16[28,896]{1,0:T(8,128)(2,1)S(1)}, bf16[28,896]{1,0:T(8,128)(2,1)S(1)}, u32[]{:S(2)}, u32[]{:S(2)}) %collective-permute-start.14) | collective-permute-done | bytes 50208 | tf_op jit(solution)/shard_map/ppermute | solution.py:86
  548.6 13.2 %add_convert_fusion = bf16[896,4864]{1,0:T(8,128)(2,1)} fusion(bf16[896,4864]{1,0:T(8,128)(2,1)} %collective-permute-done.15, bf16[512,896]{1,0:T(8,128)(2,1)S(1)} %copy-done.20, bf16[512,4864]{1,0:T(8,128)(2,1)} %get-tuple-element.77, bf16[512,4864]{1,0:T(8,128)(2,1)} %copy-done.14, pred[]{:T(512)S(6)} %eq.50), kind=kOutput, calls=%fused_computation.11 | convolution fusion | flops 4478304256 | bytes 28311552 | tf_op jit(solution)/shard_map/dot_general | solution.py:57
  561.8 4.1 fusion.84
  569.5 5.1 collective-permute-done.27
  583.0 8.6 %collective-permute-done.28 = bf16[2,152,896]{2,1,0:T(8,128)(2,1)S(1)} collective-permute-done((bf16[2,152,896]{2,1,0:T(8,128)(2,1)S(1)}, bf16[2,152,896]{2,1,0:T(8,128)(2,1)S(1)}, u32[]{:S(2)}, u32[]{:S(2)}) %collective-permute-start.28) | collective-permute-done | bytes 544800 | tf_op jit(solution)/shard_map/ppermute | solution.py:86
  595.9 22.2 %collective-permute-done.16 = bf16[2,2,2,56,2432]{4,3,2,1,0:T(8,128)(2,1)S(1)} collective-permute-done((bf16[2,2,2,56,2432]{4,3,2,1,0:T(8,128)(2,1)S(1)}, bf16[2,2,2,56,2432]{4,3,2,1,0:T(8,128)(2,1)S(1)}, u32[]{:S(2)}, u32[]{:S(2)}) %collective-permute-start.16) | collective-permute-done | bytes 2179104 | tf_op jit(solution)/shard_map/ppermute | solution.py:86
  619.3 19.0 %collective-permute-done.20 = bf16[2,2,2,56,2432]{4,3,0,2,1:T(8,128)(2,1)S(1)} collective-permute-done((bf16[2,2,2,56,2432]{4,3,0,2,1:T(8,128)(2,1)S(1)}, bf16[2,2,2,56,2432]{4,3,0,2,1:T(8,128)(2,1)S(1)}, u32[]{:S(2)}, u32[]{:S(2)}) %collective-permute-start.20) | collective-permute-done | bytes 2179104 | tf_op jit(solution)/shard_map/ppermute | solution.py:86
  641.2 13.1 %collective-permute-done.17 = bf16[2,2,56,2432]{3,2,1,0:T(8,128)(2,1)S(1)} collective-permute-done((bf16[2,2,56,2432]{3,2,1,0:T(8,128)(2,1)S(1)}, bf16[2,2,56,2432]{3,2,1,0:T(8,128)(2,1)S(1)}, u32[]{:S(2)}, u32[]{:S(2)}) %collective-permute-start.17) | collective-permute-done | bytes 1089568 | tf_op jit(solution)/shard_map/ppermute | solution.py:86
  659.5 7.4 %collective-permute-done.18 = bf16[2,56,2432]{2,1,0:T(8,128)(2,1)S(1)} collective-permute-done((bf16[2,56,2432]{2,1,0:T(8,128)(2,1)S(1)}, bf16[2,56,2432]{2,1,0:T(8,128)(2,1)S(1)}, u32[]{:S(2)}, u32[]{:S(2)}) %collective-permute-start.18) | collective-permute-done | bytes 544800 | tf_op jit(solution)/shard_map/ppermute | solution.py:86
  667.2 4.7 collective-permute-start.19
  672.8 13.4 %collective-permute-done.19 = bf16[56,2432]{1,0:T(8,128)(2,1)S(1)} collective-permute-done((bf16[56,2432]{1,0:T(8,128)(2,1)S(1)}, bf16[56,2432]{1,0:T(8,128)(2,1)S(1)}, u32[]{:S(2)}, u32[]{:S(2)}) %collective-permute-start.19) | collective-permute-done | bytes 272416 | tf_op jit(solution)/shard_map/ppermute | solution.py:86
  (328 shorter events, 154.2 us)
Async XLA Ops:
  7.2 67.7 %all-gather.4.cloned.1.call-start = ((), (), s32[]{:S(2)}) async-start(), calls=%async_computation | async-start | bytes 3852288 | tf_op jit(solution)/shard_map/all_gather | solution.py:137
  11.0 186.0 %all-gather.6.cloned.1.call-start = ((), (), s32[]{:S(2)}) async-start(), calls=%async_computation.1 | async-start | bytes 17977344 | tf_op jit(solution)/shard_map/all_gather | solution.py:157
  80.0 215.4 %all-gather.8.cloned.1.call-start = ((), (), s32[]{:S(2)}) async-start(), calls=%async_computation.2 | async-start | bytes 8988672 | tf_op jit(solution)/shard_map/all_gather | solution.py:165
  212.8 16.2 %collective-permute-start = (bf16[512,128]{1,0:T(8,128)(2,1)}, bf16[512,128]{1,0:T(8,128)(2,1)}, u32[]{:S(2)}, u32[]{:S(2)}) collective-permute-start(bf16[512,128]{1,0:T(8,128)(2,1)} %slice.178), channel_id=1, source_target_pairs={{0,1},{1,2},{2,3},{3,4},{4,5},{5,6},{6,7},{7,8},{8,9},{9,10},{10,1... | collective-permute-start | bytes 393224 | tf_op jit(solution)/shard_map/ppermute | solution.py:23
  219.5 10.7 %collective-permute-start.1 = (bf16[512,128]{1,0:T(8,128)(2,1)}, bf16[512,128]{1,0:T(8,128)(2,1)}, u32[]{:S(2)}, u32[]{:S(2)}) collective-permute-start(bf16[512,128]{1,0:T(8,128)(2,1)} %add_convert_fusion.2), channel_id=1, source_target_pairs={{0,1},{1,2},{2,3},{3,4},{4,5},{5,6},{6,7},{7,8},{8,9},{9,10},{10,1... | collective-permute-start | bytes 393224 | tf_op jit(solution)/shard_map/ppermute | solution.py:23
  420.2 29.5 %collective-permute-start.4 = (bf16[512,2,64]{0,2,1:T(8,128)(2,1)S(1)}, bf16[512,2,64]{0,2,1:T(8,128)(2,1)S(1)}, u32[]{:S(2)}, u32[]{:S(2)}) collective-permute-start(bf16[512,2,64]{0,2,1:T(8,128)(2,1)S(1)} %slice.176), channel_id=1, source_target_pairs={{1,0},{2,1},{3,2},{4,3},{5,4},{6,5},{7,6},{8,7},{9,8},{10,9},{11,1... | collective-permute-start | bytes 393224 | tf_op jit(solution)/shard_map/ppermute | solution.py:23
  428.0 43.4 %collective-permute-start.10 = (bf16[2,2,2,2,28,896]{5,3,4,2,1,0:T(2,128)(2,1)}, bf16[2,2,2,2,28,896]{5,3,4,2,1,0:T(2,128)(2,1)}, u32[]{:S(2)}, u32[]{:S(2)}) collective-permute-start(bf16[2,2,2,2,28,896]{5,3,4,2,1,0:T(2,128)(2,1)} %bitcast.247), channel_id=1, source_target_pairs={{0,1},{1,0},{2,3},{3,2},{4,5},{5,4},{6,7},{7,6},{8,9},{9,8},{10,11... | collective-permute-start | bytes 2408456 | tf_op jit(solution)/shard_map/ppermute | solution.py:86
  441.9 45.3 %collective-permute-start.25 = (bf16[16,152,896]{2,1,0:T(8,128)(2,1)}, bf16[16,152,896]{2,1,0:T(8,128)(2,1)}, u32[]{:S(2)}, u32[]{:S(2)}) collective-permute-start(bf16[16,152,896]{2,1,0:T(8,128)(2,1)} %dynamic-slice_bitcast_fusion), channel_id=1, source_target_pairs={{0,1},{1,0},{2,3},{3,2},{4,5},{5,4},{6,7},{7,6},{8,9},{9,8},{10,11... | collective-permute-start | bytes 13074440 | tf_op jit(solution)/shard_map/ppermute | solution.py:86
  441.9 106.5 %collective-permute-start.15 = (bf16[896,4864]{1,0:T(8,128)(2,1)}, bf16[896,4864]{1,0:T(8,128)(2,1)}, u32[]{:S(2)}, u32[]{:S(2)}) collective-permute-start(bf16[896,4864]{1,0:T(8,128)(2,1)} %convolution_convert_fusion.1), channel_id=1, source_target_pairs={{0,1},{1,0},{2,3},{3,2},{4,5},{5,4},{6,7},{7,6},{8,9},{9,8},{10,11... | collective-permute-start | bytes 26148872 | tf_op jit(solution)/shard_map/ppermute | solution.py:86
  442.4 7.2 %collective-permute-start.3 = (bf16[512,2,64]{0,2,1:T(8,128)(2,1)S(1)}, bf16[512,2,64]{0,2,1:T(8,128)(2,1)S(1)}, u32[]{:S(2)}, u32[]{:S(2)}) collective-permute-start(bf16[512,2,64]{0,2,1:T(8,128)(2,1)S(1)} %slice.177), channel_id=1, source_target_pairs={{1,0},{2,1},{3,2},{4,3},{5,4},{6,5},{7,6},{8,7},{9,8},{10,9},{11,1... | collective-permute-start | bytes 393224 | tf_op jit(solution)/shard_map/ppermute | solution.py:23
  460.1 14.6 %collective-permute-start.5 = (bf16[2,2,2,2,29,1152]{5,3,4,2,1,0:T(2,128)(2,1)S(1)}, bf16[2,2,2,2,29,1152]{5,3,4,2,1,0:T(2,128)(2,1)S(1)}, u32[]{:S(2)}, u32[]{:S(2)}) collective-permute-start(bf16[2,2,2,2,29,1152]{5,3,4,2,1,0:T(2,128)(2,1)S(1)} %bitcast.285), channel_id=1, source_target_pairs={{0,1},{1,0},{2,3},{3,2},{4,5},{5,4},{6,7},{7,6},{8,9},{9,8},{10,11... | collective-permute-start | bytes 3207176 | tf_op jit(solution)/shard_map/ppermute | solution.py:86
  472.9 12.6 %collective-permute-start.11 = (bf16[2,2,2,28,896]{4,3,2,1,0:T(8,128)(2,1)S(1)}, bf16[2,2,2,28,896]{4,3,2,1,0:T(8,128)(2,1)S(1)}, u32[]{:S(2)}, u32[]{:S(2)}) collective-permute-start(bf16[2,2,2,28,896]{4,3,2,1,0:T(8,128)(2,1)S(1)} %dynamic-slice_bitcast_fusion.10), channel_id=1, source_target_pairs={{0,4},{1,5},{2,6},{3,7},{4,0},{5,1},{6,2},{7,3},{8,12},{9,13},{10,... | collective-permute-start | bytes 1204232 | tf_op jit(solution)/shard_map/ppermute | solution.py:86
  485.7 8.3 %collective-permute-start.12 = (bf16[2,2,28,896]{3,2,1,0:T(8,128)(2,1)S(1)}, bf16[2,2,28,896]{3,2,1,0:T(8,128)(2,1)S(1)}, u32[]{:S(2)}, u32[]{:S(2)}) collective-permute-start(bf16[2,2,28,896]{3,2,1,0:T(8,128)(2,1)S(1)} %dynamic-slice_bitcast_fusion.15), channel_id=1, source_target_pairs={{0,8},{1,9},{2,10},{3,11},{4,12},{5,13},{6,14},{7,15},{8,0},{9,1},... | collective-permute-start | bytes 602120 | tf_op jit(solution)/shard_map/ppermute | solution.py:86
  493.4 51.2 %collective-permute-start.26 = (bf16[2,2,2,152,896]{4,3,2,1,0:T(8,128)(2,1)}, bf16[2,2,2,152,896]{4,3,2,1,0:T(8,128)(2,1)}, u32[]{:S(2)}, u32[]{:S(2)}) collective-permute-start(bf16[2,2,2,152,896]{4,3,2,1,0:T(8,128)(2,1)} %dynamic-slice_bitcast_fusion.1), channel_id=1, source_target_pairs={{0,8},{1,9},{2,10},{3,11},{4,12},{5,13},{6,14},{7,15},{8,0},{9,1},... | collective-permute-start | bytes 6537224 | tf_op jit(solution)/shard_map/ppermute | solution.py:86
  494.1 6.1 collective-permute-start.13
  495.9 46.0 %collective-permute-start.6 = (bf16[2,2,2,29,1152]{4,2,3,1,0:T(2,128)(2,1)S(1)}, bf16[2,2,2,29,1152]{4,2,3,1,0:T(2,128)(2,1)S(1)}, u32[]{:S(2)}, u32[]{:S(2)}) collective-permute-start(bf16[2,2,2,29,1152]{4,2,3,1,0:T(2,128)(2,1)S(1)} %bitcast.291), channel_id=1, source_target_pairs={{0,2},{1,3},{2,0},{3,1},{4,6},{5,7},{6,4},{7,5},{8,10},{9,11},{10,... | collective-permute-start | bytes 1603592 | tf_op jit(solution)/shard_map/ppermute | solution.py:86
  500.2 41.1 %collective-permute-start.14 = (bf16[28,896]{1,0:T(8,128)(2,1)S(1)}, bf16[28,896]{1,0:T(8,128)(2,1)S(1)}, u32[]{:S(2)}, u32[]{:S(2)}) collective-permute-start(bf16[28,896]{1,0:T(8,128)(2,1)S(1)} %dynamic-slice_bitcast_fusion.19), channel_id=1, source_target_pairs={{0,16},{1,17},{2,18},{3,19},{4,20},{5,21},{6,22},{7,23},{8,24},{9,... | collective-permute-start | bytes 150536 | tf_op jit(solution)/shard_map/ppermute | solution.py:86
  542.8 24.3 %collective-permute-start.7 = (bf16[2,2,29,1152]{3,2,1,0:T(8,128)(2,1)}, bf16[2,2,29,1152]{3,2,1,0:T(8,128)(2,1)S(1)}, u32[]{:S(2)}, u32[]{:S(2)}) collective-permute-start(bf16[2,2,29,1152]{3,2,1,0:T(8,128)(2,1)} %dynamic-slice_bitcast_fusion.11), channel_id=1, source_target_pairs={{0,4},{1,5},{2,6},{3,7},{4,0},{5,1},{6,2},{7,3},{8,12},{9,13},{10,... | collective-permute-start | bytes 801800 | tf_op jit(solution)/shard_map/ppermute | solution.py:86
  547.5 27.1 %collective-permute-start.27 = (bf16[2,2,152,896]{3,2,1,0:T(8,128)(2,1)S(1)}, bf16[2,2,152,896]{3,2,1,0:T(8,128)(2,1)}, u32[]{:S(2)}, u32[]{:S(2)}) collective-permute-start(bf16[2,2,152,896]{3,2,1,0:T(8,128)(2,1)S(1)} %dynamic-slice_bitcast_fusion.3), channel_id=1, source_target_pairs={{0,2},{1,3},{2,0},{3,1},{4,6},{5,7},{6,4},{7,5},{8,10},{9,11},{10,... | collective-permute-start | bytes 3268616 | tf_op jit(solution)/shard_map/ppermute | solution.py:86
  566.0 52.0 %collective-permute-start.16 = (bf16[2,2,2,56,2432]{4,3,2,1,0:T(8,128)(2,1)S(1)}, bf16[2,2,2,56,2432]{4,3,2,1,0:T(8,128)(2,1)S(1)}, u32[]{:S(2)}, u32[]{:S(2)}) collective-permute-start(bf16[2,2,2,56,2432]{4,3,2,1,0:T(8,128)(2,1)S(1)} %dynamic-slice_bitcast_fusion.2), channel_id=1, source_target_pairs={{0,2},{1,3},{2,0},{3,1},{4,6},{5,7},{6,4},{7,5},{8,10},{9,11},{10,... | collective-permute-start | bytes 6537224 | tf_op jit(solution)/shard_map/ppermute | solution.py:86
  567.2 11.7 %collective-permute-start.8 = (bf16[2,29,1152]{2,1,0:T(8,128)(2,1)S(1)}, bf16[2,29,1152]{2,1,0:T(8,128)(2,1)S(1)}, u32[]{:S(2)}, u32[]{:S(2)}) collective-permute-start(bf16[2,29,1152]{2,1,0:T(8,128)(2,1)S(1)} %dynamic-slice_bitcast_fusion.16), channel_id=1, source_target_pairs={{0,8},{1,9},{2,10},{3,11},{4,12},{5,13},{6,14},{7,15},{8,0},{9,1},... | collective-permute-start | bytes 400904 | tf_op jit(solution)/shard_map/ppermute | solution.py:86
  576.2 15.4 %collective-permute-start.28 = (bf16[2,152,896]{2,1,0:T(8,128)(2,1)S(1)}, bf16[2,152,896]{2,1,0:T(8,128)(2,1)S(1)}, u32[]{:S(2)}, u32[]{:S(2)}) collective-permute-start(bf16[2,152,896]{2,1,0:T(8,128)(2,1)S(1)} %dynamic-slice_bitcast_fusion.7), channel_id=1, source_target_pairs={{0,4},{1,5},{2,6},{3,7},{4,0},{5,1},{6,2},{7,3},{8,12},{9,13},{10,... | collective-permute-start | bytes 1634312 | tf_op jit(solution)/shard_map/ppermute | solution.py:86
  577.1 61.2 %collective-permute-start.20 = (bf16[2,2,2,56,2432]{4,3,0,2,1:T(8,128)(2,1)S(1)}, bf16[2,2,2,56,2432]{4,3,0,2,1:T(8,128)(2,1)S(1)}, u32[]{:S(2)}, u32[]{:S(2)}) collective-permute-start(bf16[2,2,2,56,2432]{4,3,0,2,1:T(8,128)(2,1)S(1)} %bitcast.278), channel_id=1, source_target_pairs={{0,4},{1,5},{2,6},{3,7},{4,0},{5,1},{6,2},{7,3},{8,12},{9,13},{10,... | collective-permute-start | bytes 6537224 | tf_op jit(solution)/shard_map/ppermute | solution.py:86
  579.6 110.6 %collective-permute-start.9 = (bf16[29,1152]{1,0:T(8,128)(2,1)}, bf16[29,1152]{1,0:T(8,128)(2,1)}, u32[]{:S(2)}, u32[]{:S(2)}) collective-permute-start(bf16[29,1152]{1,0:T(8,128)(2,1)} %dynamic-slice_bitcast_fusion.18), channel_id=1, source_target_pairs={{0,16},{1,17},{2,18},{3,19},{4,20},{5,21},{6,22},{7,23},{8,24},{9,... | collective-permute-start | bytes 200456 | tf_op jit(solution)/shard_map/ppermute | solution.py:86
  592.5 100.5 %collective-permute-start.29 = (bf16[152,896]{1,0:T(8,128)(2,1)}, bf16[152,896]{1,0:T(8,128)(2,1)}, u32[]{:S(2)}, u32[]{:S(2)}) collective-permute-start(bf16[152,896]{1,0:T(8,128)(2,1)} %dynamic-slice_bitcast_fusion.12), channel_id=1, source_target_pairs={{0,16},{1,17},{2,18},{3,19},{4,20},{5,21},{6,22},{7,23},{8,24},{9,... | collective-permute-start | bytes 817160 | tf_op jit(solution)/shard_map/ppermute | solution.py:86
  618.7 35.7 %collective-permute-start.17 = (bf16[2,2,56,2432]{3,2,1,0:T(8,128)(2,1)S(1)}, bf16[2,2,56,2432]{3,2,1,0:T(8,128)(2,1)S(1)}, u32[]{:S(2)}, u32[]{:S(2)}) collective-permute-start(bf16[2,2,56,2432]{3,2,1,0:T(8,128)(2,1)S(1)} %dynamic-slice_bitcast_fusion.5), channel_id=1, source_target_pairs={{0,4},{1,5},{2,6},{3,7},{4,0},{5,1},{6,2},{7,3},{8,12},{9,13},{10,... | collective-permute-start | bytes 3268616 | tf_op jit(solution)/shard_map/ppermute | solution.py:86
  638.9 20.2 %collective-permute-start.21 = (bf16[2,2,56,2432]{3,2,0,1:T(8,128)(2,1)S(1)}, bf16[2,2,56,2432]{3,2,0,1:T(8,128)(2,1)S(1)}, u32[]{:S(2)}, u32[]{:S(2)}) collective-permute-start(bf16[2,2,56,2432]{3,2,0,1:T(8,128)(2,1)S(1)} %dynamic-slice_bitcast_fusion.4), channel_id=1, source_target_pairs={{0,8},{1,9},{2,10},{3,11},{4,12},{5,13},{6,14},{7,15},{8,0},{9,1},... | collective-permute-start | bytes 3268616 | tf_op jit(solution)/shard_map/ppermute | solution.py:86
  654.7 12.3 %collective-permute-start.18 = (bf16[2,56,2432]{2,1,0:T(8,128)(2,1)S(1)}, bf16[2,56,2432]{2,1,0:T(8,128)(2,1)S(1)}, u32[]{:S(2)}, u32[]{:S(2)}) collective-permute-start(bf16[2,56,2432]{2,1,0:T(8,128)(2,1)S(1)} %dynamic-slice_bitcast_fusion.9), channel_id=1, source_target_pairs={{0,8},{1,9},{2,10},{3,11},{4,12},{5,13},{6,14},{7,15},{8,0},{9,1},... | collective-permute-start | bytes 1634312 | tf_op jit(solution)/shard_map/ppermute | solution.py:86
  659.5 12.4 %collective-permute-start.22 = (bf16[2,56,2432]{2,1,0:T(8,128)(2,1)S(1)}, bf16[2,56,2432]{2,1,0:T(8,128)(2,1)S(1)}, u32[]{:S(2)}, u32[]{:S(2)}) collective-permute-start(bf16[2,56,2432]{2,1,0:T(8,128)(2,1)S(1)} %dynamic-slice_bitcast_fusion.8), channel_id=1, source_target_pairs={{0,2},{1,3},{2,0},{3,1},{4,6},{5,7},{6,4},{7,5},{8,10},{9,11},{10,... | collective-permute-start | bytes 1634312 | tf_op jit(solution)/shard_map/ppermute | solution.py:86
  667.2 19.0 %collective-permute-start.19 = (bf16[56,2432]{1,0:T(8,128)(2,1)S(1)}, bf16[56,2432]{1,0:T(8,128)(2,1)S(1)}, u32[]{:S(2)}, u32[]{:S(2)}) collective-permute-start(bf16[56,2432]{1,0:T(8,128)(2,1)S(1)} %dynamic-slice_bitcast_fusion.14), channel_id=1, source_target_pairs={{0,16},{1,17},{2,18},{3,19},{4,20},{5,21},{6,22},{7,23},{8,24},{9,... | collective-permute-start | bytes 817160 | tf_op jit(solution)/shard_map/ppermute | solution.py:86
  672.1 17.0 %collective-permute-start.23 = (bf16[56,2432]{1,0:T(8,128)(2,1)S(1)}, bf16[56,2432]{1,0:T(8,128)(2,1)S(1)}, u32[]{:S(2)}, u32[]{:S(2)}) collective-permute-start(bf16[56,2432]{1,0:T(8,128)(2,1)S(1)} %dynamic-slice_bitcast_fusion.13), channel_id=1, source_target_pairs={{0,16},{1,17},{2,18},{3,19},{4,20},{5,21},{6,22},{7,23},{8,24},{9,... | collective-permute-start | bytes 817160 | tf_op jit(solution)/shard_map/ppermute | solution.py:86
  690.2 4.6 collective-permute-start.24
  (65 other events, 1025.3 us)
Sparse Core Ops, SparseCore 0:
  11.5 63.2 all-gather.3
  80.2 116.8 all-gather.5
  200.0 76.9 all-gather.7

commit v2 on v1

--- a/solution.py
+++ b/solution.py
@@ -97,15 +97,20 @@
     return kept.astype(jnp.float32) + partner_swap(sent, bit).astype(jnp.float32)
 
 
-def reduce_to_owner(x, bits, order):
+def reduce_step(x, bits, order, upto):
     left = list(bits)
     x = x.reshape((2,) * len(left) + x.shape[1:])
-    for bit in order:
+    for bit in order[:upto]:
         x = halve(x, left.index(bit), bit)
         left.remove(bit)
         if left:
             x = x.astype(jnp.bfloat16)
-    return x
+    x = x.reshape((-1,) + x.shape[len(left) :]) if left else x
+    return (x, tuple(left), tuple(order[upto:]))
+
+
+def reduce_to_owner(x, bits, order):
+    return reduce_step(x, bits, order, len(order))[0]
 
 
 def norm_back(grad_normed, hidden, factor, gain):
@@ -161,8 +166,6 @@
     else:
         gu_all = lax.all_gather(w_gate_up, "fsdp", axis=0, tiled=True).reshape(width, 2 * FF)
         wgate, wup = gu_all[:, :FF], gu_all[:, FF:]
-    down_own, gu_all = lax.optimization_barrier((w_down.reshape(FF // n_devices, width), gu_all))
-    wdown = lax.all_gather(down_own, "fsdp", axis=0, tiled=True)
     base_index = lax.axis_index("fsdp") * tok_rows
     token_index, segment, position = segment_info(lengths, base_index, tok_rows)
     prev_index, prev_segment, unused_pos = segment_info(lengths, base_index - tok_rows, tok_rows)
@@ -181,6 +184,8 @@
     )
     keyed = keyed.astype(jnp.bfloat16).reshape(tok_rows, kv_dim)
     valued = linear[:, query_dim + kv_dim :].astype(jnp.bfloat16)
+    down_own, keyed = lax.optimization_barrier((w_down.reshape(FF // n_devices, width), keyed))
+    wdown = lax.all_gather(down_own, "fsdp", axis=0, tiled=True)
     key_prev, value_prev = passed_along((keyed, valued), "fsdp", 1)
     key_all = jnp.concatenate([key_prev, keyed]).reshape(2 * tok_rows, KV_HEADS, HD)
     value_all = jnp.concatenate([value_prev, valued]).reshape(2 * tok_rows, KV_HEADS, HD)
@@ -225,79 +230,71 @@
     far = bits[: len(bits) - 4]
     grad_down = outer_sum(product, grad_out).astype(jnp.bfloat16)
     down_parts = halve(grad_down.reshape(chips, 2, -1, width), 1, 0).astype(jnp.bfloat16)
-    down_sum = reduce_to_owner(down_parts, bits[:-1], (3, 1, 2) + far)
     grad_product = back_dot(grad_out, wdown)
     grad_gate = grad_product * up_pre * sigma * (1.0 + gate_pre * (1.0 - sigma))
     grad_up = grad_product * silu_gate
     grad_gate = grad_gate.astype(jnp.bfloat16)
     grad_up = grad_up.astype(jnp.bfloat16)
+    chip_bits = bits[:-1]
+    moving = [(down_parts, chip_bits, (3, 1, 2) + far)]
     if whole_rows:
         gu_sent = outer_sum(normed_two, jnp.where(core == 0, grad_up, grad_gate))
         gu_came = partner_swap(gu_sent.astype(jnp.bfloat16), 0)
         gu_kept = outer_sum(normed_two, jnp.where(core == 0, grad_gate, grad_up))
-        gu_parts = (gu_kept + gu_came.astype(jnp.float32)).astype(jnp.bfloat16)
-        gu_parts = gu_parts.reshape(chips, 2 * rows_own, FF)
-        gu_sums = (
-            reduce_to_owner(gu_parts[:, :, : FF // 2], bits[:-1], (1, 2, 3) + far),
-            reduce_to_owner(gu_parts[:, :, FF // 2 :], bits[:-1], (2, 3, 1) + far),
-        )
-        gu_sum = jnp.concatenate(gu_sums, axis=1).reshape(2, rows_own, FF)
-        gu_kept = lax.dynamic_index_in_dim(gu_sum, core, 0, keepdims=False)
-        gu_came = partner_swap(lax.dynamic_index_in_dim(gu_sum, 1 - core, 0, keepdims=False), 0)
-        grad_wgu = jnp.concatenate(
-            [jnp.where(core == 0, gu_kept, gu_came), jnp.where(core == 0, gu_came, gu_kept)], axis=1
-        )
+        gu_kept = gu_kept.astype(jnp.bfloat16)
     else:
         grad_gu = jnp.concatenate([grad_gate, grad_up], axis=1)
         gu_parts = outer_sum(normed_two, grad_gu).astype(jnp.bfloat16)
-        grad_wgu = reduce_to_owner(gu_parts.reshape(n_devices, -1), bits, (0, 1, 2, 3) + far)
+        moving.append((gu_parts.reshape(n_devices, -1), bits, (0, 1, 2, 3) + far))
     grad_normed_two = back_dot(grad_gate, wgate) + back_dot(grad_up, wup)
     grad_middle_norm, grad_gain_two = norm_back(grad_normed_two, middle, factor_two, gain_two)
     grad_middle = grad_out.astype(jnp.float32) + grad_middle_norm
     grad_branch = grad_middle.astype(jnp.bfloat16)
+    if whole_rows:
+        grad_branch, gu_kept, gu_came, down_parts = lax.optimization_barrier(
+            (grad_branch, gu_kept, gu_came, down_parts)
+        )
+        gu_parts = (gu_kept.astype(jnp.float32) + gu_came.astype(jnp.float32)).astype(jnp.bfloat16)
+        gu_parts = gu_parts.reshape(chips, 2 * rows_own, FF)
+        moving = [
+            (down_parts, chip_bits, (3, 1, 2) + far),
+            (gu_parts[:, :, : FF // 2], chip_bits, (1, 2, 3) + far),
+            (gu_parts[:, :, FF // 2 :], chip_bits, (2, 3, 1) + far),
+        ]
     grad_wout = outer_sum(attended, grad_branch).astype(jnp.bfloat16)
-    wout_sum = reduce_to_owner(
-        grad_wout.reshape((n_devices, -1, width) if whole_rows else (n_devices, -1)),
-        bits,
-        (0, 2, 3, 1) + far,
-    )
+    grad_wout = grad_wout.reshape((n_devices, -1, width) if whole_rows else (n_devices, -1))
+    moving.append((grad_wout, bits, (0, 2, 3, 1) + far))
+
+    def one_step(moving, held):
+        stepped = [reduce_step(*part, 1) for part in moving]
+        held, sums = lax.optimization_barrier((held, [part[0] for part in stepped]))
+        return ([(x,) + part[1:] for x, part in zip(sums, stepped)], held)
+
     grad_att = back_dot(grad_branch, wout).astype(jnp.bfloat16)
     grad_att_four = grad_att.reshape(tok_rows, KV_HEADS, groups, HD)
 
-    def back_block(number, carried):
-        grad_query, grad_key, grad_value = carried
-        rows_q, key_block, value_block, scores = scores_of()
-        probs = jnp.exp(scores - log_sums[number])
-        grad_probs = jnp.einsum(
-            "qkgd,jkd->kgqj", grad_att_four, value_block, preferred_element_type=jnp.float32
-        )
-        inner = jnp.sum(probs * grad_probs, axis=-1, keepdims=True)
-        grad_scores = (probs * (grad_probs - inner)).astype(jnp.bfloat16)
-        part_query = (
-            jnp.einsum("kgqj,jkd->qkgd", grad_scores, key_block, preferred_element_type=jnp.float32)
-            * scale
-        )
-        part_key = (
-            jnp.einsum("kgqj,qkgd->jkd", grad_scores, rows_q, preferred_element_type=jnp.float32)
-            * scale
-        )
-        part_value = jnp.einsum(
-            "kgqj,qkgd->jkd",
-            probs.astype(jnp.bfloat16),
-            grad_att_four,
-            preferred_element_type=jnp.float32,
-        )
-        grad_query = part_query
-        grad_key = grad_key + part_key
-        grad_value = grad_value + part_value
-        return (grad_query, grad_key, grad_value)
-
-    start_state = (
-        jnp.zeros((tok_rows, KV_HEADS, groups, HD), jnp.float32),
-        jnp.zeros((2 * tok_rows, KV_HEADS, HD), jnp.float32),
-        jnp.zeros((2 * tok_rows, KV_HEADS, HD), jnp.float32),
-    )
-    grad_query, grad_key, grad_value = lax.fori_loop(0, block_count, back_block, start_state)
+    rows_q, key_block, value_block, scores = scores_of()
+    probs = jnp.exp(scores - log_sums[0])
+    grad_probs = jnp.einsum(
+        "qkgd,jkd->kgqj", grad_att_four, value_block, preferred_element_type=jnp.float32
+    )
+    inner = jnp.sum(probs * grad_probs, axis=-1, keepdims=True)
+    moving, inner = one_step(moving, inner)
+    grad_scores = (probs * (grad_probs - inner)).astype(jnp.bfloat16)
+    grad_key = (
+        jnp.einsum("kgqj,qkgd->jkd", grad_scores, rows_q, preferred_element_type=jnp.float32)
+        * scale
+    )
+    grad_value = jnp.einsum(
+        "kgqj,qkgd->jkd",
+        probs.astype(jnp.bfloat16),
+        grad_att_four,
+        preferred_element_type=jnp.float32,
+    )
+    grad_query = (
+        jnp.einsum("kgqj,jkd->qkgd", grad_scores, key_block, preferred_element_type=jnp.float32)
+        * scale
+    )
     key_back, value_back = (
         passed_along(grad_key[:tok_rows].astype(jnp.bfloat16), "fsdp", -1).astype(jnp.float32),
         passed_along(grad_value[:tok_rows].astype(jnp.bfloat16), "fsdp", -1).astype(jnp.float32),
@@ -311,6 +308,7 @@
     grad_linear = jnp.concatenate([grad_query_lin, grad_key_lin, grad_value_own], axis=1).astype(
         jnp.bfloat16
     )
+    moving, grad_linear = one_step(moving, grad_linear)
     grad_wqkv = outer_sum(normed_one, grad_linear)
     grad_bias = jnp.sum(grad_linear.astype(jnp.float32), axis=0)
     grad_normed_one = back_dot(grad_linear, wqkv)
@@ -330,6 +328,18 @@
     last = jnp.concatenate([grad_wqkv, vectors], axis=1).astype(jnp.bfloat16)
     last_sum = reduce_to_owner(last, bits, (0, 1, 2, 3) + far).reshape(-1)
     qkv_own = w_qkv.shape[0]
+    sums = [reduce_to_owner(*part) for part in moving]
+    down_sum, wout_sum = sums[0], sums[-1]
+    if whole_rows:
+        gu_sum = jnp.concatenate(sums[1:3], axis=1).reshape(2, rows_own, FF)
+        gu_kept = lax.dynamic_index_in_dim(gu_sum, core, 0, keepdims=False)
+        gu_came = partner_swap(lax.dynamic_index_in_dim(gu_sum, 1 - core, 0, keepdims=False), 0)
+        grad_wgu = jnp.concatenate(
+            [jnp.where(core == 0, gu_kept, gu_came), jnp.where(core == 0, gu_came, gu_kept)],
+            axis=1,
+        )
+    else:
+        grad_wgu = sums[1]
     return (
         output,
         grad_tokens,

time: 711 us -> 686 us (0.965)
  waiting for transfers between devices: 324 us -> 263 us
  other arithmetic: 65.6 us -> 100 us
  local copies, waits for them, and re-layouts: 66.9 us -> 81 us
  starting transfers between devices: 45.7 us -> 37.6 us
    all_gather x1, waiting for transfers between devices: 116 us -> 38.3 us  [local(): gu_all = lax.all_gather(gu_chip, 'fsdp', axis=0, tiled=True)]
    all_gather x1, waiting for transfers between devices: 0.01 us -> 56.2 us  [local(): wdown = lax.all_gather(down_own, 'fsdp', axis=0, tiled=True)]
    ppermute x26, waiting for transfers between devices: 146 us -> 110 us  [partner_swap(): return lax.ppermute(x, 'fsdp', [(i, i ^ 1 << bit) for i in range(peers)])]
    convert_element_type x18 -> x20, other arithmetic: 33.7 us -> 60.3 us  [the longest x1 25.3 us: local(): grad_scores = (probs * (grad_probs - inner)).astype(jnp.bfloat16)]
    squeeze x19 -> x20, local copies, waits for them, and re-layouts: 7.17 us -> 14.9 us  [halve(): lax.dynamic_index_in_dim(x, 1 - mine, axis, keepdims=False)]
    ppermute x26, starting transfers between devices: 36.3 us -> 28.7 us  [partner_swap(): return lax.ppermute(x, 'fsdp', [(i, i ^ 1 << bit) for i in range(peers)])]
  transfers between devices with their start and end apart: 33 -> 33, of which waited for: 16 -> 16; matrix products, arithmetic and copies ran while one was open for 25% -> 35% of each run, Pallas kernels for 0% -> 0%
where the time goes in v2:
time: 686 us; the launch traced here: 678 us
  waiting for transfers between devices  263 us (38%)
  matrix products  181 us (26%)
  other arithmetic  100 us (15%)
  local copies, waits for them, and re-layouts  81 us (12%)
  starting transfers between devices  37.6 us (5%)
  between operations  15.3 us (2%)
    ppermute x26, waiting for transfers between devices, partner_swap(): return lax.ppermute(x, 'fsdp', [(i, i ^ 1 << bit) for i in range(peers)])  110 us
    all_gather x1, waiting for transfers between devices, local(): lax.all_gather(attn_flat, 'fsdp', axis=0, tiled=True).reshape(n_devices, -1)  57.9 us
    all_gather x1, waiting for transfers between devices, local(): wdown = lax.all_gather(down_own, 'fsdp', axis=0, tiled=True)  56.2 us
    dot_general x5, matrix products, back_dot(): lax.dot_general(left, right, (((1,), (1,)), ((), ())), preferred_element_...  42.1 us
    all_gather x1, waiting for transfers between devices, local(): gu_all = lax.all_gather(gu_chip, 'fsdp', axis=0, tiled=True)  38.3 us
    dot_general x5, matrix products, outer_sum(): lax.dot_general(left, right, (((0,), (0,)), ((), ())), preferred_element_...  31.8 us
    ppermute x26, starting transfers between devices, partner_swap(): return lax.ppermute(x, 'fsdp', [(i, i ^ 1 << bit) for i in range(peers)])  28.7 us
    convert_element_type x1, other arithmetic, local(): grad_scores = (probs * (grad_probs - inner)).astype(jnp.bfloat16)  25.3 us
  transfers between devices with their start and end apart: 33, of which 16 were waited for; matrix products, arithmetic and copies ran while one was open for 35% of the time, Pallas kernels for 0%

profile of v2, /device:TPU:0, one launch (start us, length us, event | category | flops | bytes accessed | tf_op | source)
XLA Modules:
  0.0 678.2 jit_solution(4669094449634894383)
XLA Ops:
  16.9 57.9 %all-gather.4.cloned.1.call-done = bf16[1867776]{0:T(1024)(128)(2,1)} async-done(((bf16[58368]{0:T(1024)(128)(2,1)}), bf16[1867776]{0:T(1024)(128)(2,1)}) %all-gather.4.cloned.1.call-update) | async-done | bytes 3735568 | tf_op jit(solution)/shard_map/all_gather | solution.py:142
  119.2 12.0 %fusion.77 = (f32[2,7,512]{2,1,0:T(8,128)S(1)}, f32[2,7,512,1024]{2,3,1,0:T(8,128)}) fusion(bf16[1024,2,64,1]{0,2,3,1:T(8,128)(2,1)S(1)} %bitcast.303, bf16[512,2,7,64]{0,3,2,1:T(8,128)(2,1)S(1)} %fusion.38, pred[512,1024]{0,1:T(8,128)(4,1)S(1)} %and_and_fusion), kind=kOutput, calls=%fused_computation.204 | convolution fusion | flops 961537024 | bytes 31092736 | tf_op jit(solution)/shard_map/while/body/eval_jaxpr/qkgd,jkd->kgqj/dot_general | solution.py:201
  131.2 11.7 %fusion.3 = f32[2,7,512]{2,1,0:T(8,128)S(1)} fusion(f32[2,7,512,1024]{2,3,1,0:T(8,128)} %get-tuple-element.103, f32[2,7,512]{2,1,0:T(8,128)S(1)} %get-tuple-element.102), kind=kLoop, calls=%fused_computation.9 | loop fusion | flops 14672896 | bytes 29417472 | tf_op jit(solution)/shard_map/while/body/eval_jaxpr/reduce_sum | solution.py:211
  142.9 14.3 %fusion.42 = bf16[2,64,7,512]{3,1,2,0:T(8,128)(2,1)S(1)} fusion(bf16[1024,2,64,1]{0,2,3,1:T(8,128)(2,1)S(1)} %bitcast.307, f32[2,7,512,1024]{2,3,1,0:T(8,128)} %get-tuple-element.103, f32[2,7,512]{2,1,0:T(8,128)S(1)} %fusion.3, f32[2,7,512]{2,1,0:T(8,128)S(1)} %get-tuple-element.102), kind=kOutput, calls=%fused_computation.91 | convolution fusion | flops 962002944 | bytes 30597120 | tf_op jit(solution)/shard_map/while/body/eval_jaxpr/kgqj,jkd->qkgd/dot_general | solution.py:213
  160.2 38.3 %all-gather.6.cloned.1.call-done = bf16[1792,4864]{1,0:T(8,128)(2,1)} async-done(((bf16[56,4864]{1,0:T(8,128)(2,1)}), bf16[1792,4864]{1,0:T(8,128)(2,1)}) %all-gather.6.cloned.1.call-update) | async-done | bytes 17432592 | tf_op jit(solution)/shard_map/all_gather | solution.py:162
  198.5 6.6 fusion.75
  205.2 8.6 %fusion.79 = f32[512,4864]{1,0:T(8,128)} fusion(bf16[512,896]{1,0:T(8,128)(2,1)S(1)} %multiply_convert_fusion.1, bf16[896,4864]{1,0:T(8,128)(2,1)S(1)} %bitcast.295), kind=kOutput, calls=%fused_computation.206 | convolution fusion | flops 4462739456 | bytes 19595264 | tf_op jit(solution)/shard_map/dot_general | solution.py:222
  214.3 8.2 %fusion.78 = f32[512,4864]{1,0:T(8,128)} fusion(bf16[512,896]{1,0:T(8,128)(2,1)S(1)} %multiply_convert_fusion.1, bf16[896,4864]{1,0:T(8,128)(2,1)S(1)} %bitcast.297), kind=kOutput, calls=%fused_computation.205 | convolution fusion | flops 4462739456 | bytes 19595264 | tf_op jit(solution)/shard_map/dot_general | solution.py:221
  222.6 56.2 %all-gather.8.cloned.1.call-done = bf16[4864,896]{1,0:T(8,128)(2,1)} async-done(((bf16[152,896]{1,0:T(8,128)(2,1)}), bf16[4864,896]{1,0:T(8,128)(2,1)}) %all-gather.8.cloned.1.call-update) | async-done | bytes 8716304 | tf_op jit(solution)/shard_map/all_gather | solution.py:188
  278.8 16.9 %fusion.12 = (bf16[512,4864]{1,0:T(8,128)(2,1)S(1)}, bf16[512,4864]{1,0:T(8,128)(2,1)}, bf16[512,4864]{1,0:T(8,128)(2,1)}) fusion(f32[512,4864]{1,0:T(8,128)} %fusion.78, f32[512,4864]{1,0:T(8,128)} %fusion.79, bf16[4864,896]{1,0:T(8,128)(2,1)} %all-gather.8.cloned.1.call-done, bf16[512,896]{1,0:T(8,128)(2,1)} %param.17), kind=kOutput, calls=%fused_computation.20 | convolution fusion | flops 4500094976 | bytes 44498944 | tf_op jit(solution)/shard_map/dot_general | solution.py:63
  295.7 10.1 %convolution_convert_fusion.1 = bf16[896,4864]{1,0:T(8,128)(2,1)} fusion(bf16[512,896]{1,0:T(8,128)(2,1)} %copy-done.16, bf16[512,4864]{1,0:T(8,128)(2,1)S(1)} %get-tuple-element.79, bf16[512,4864]{1,0:T(8,128)(2,1)} %get-tuple-element.80, pred[]{:T(512)S(6)} %eq.43), kind=kOutput, calls=%fused_computation.25 | convolution fusion | flops 4469587968 | bytes 19595264 | tf_op jit(solution)/shard_map/dot_general | solution.py:57
  308.8 7.9 %convolution_convert_fusion = bf16[4864,896]{1,0:T(8,128)(2,1)S(1)} fusion(bf16[512,4864]{1,0:T(8,128)(2,1)} %get-tuple-element.81, bf16[512,896]{1,0:T(8,128)(2,1)} %param.17), kind=kOutput, calls=%fused_computation.24 | convolution fusion | flops 4467097600 | bytes 14614528 | tf_op jit(solution)/shard_map/dot_general | solution.py:57
  322.4 10.5 %fusion.80 = f32[512,896]{1,0:T(8,128)S(1)} fusion(bf16[512,4864]{1,0:T(8,128)(2,1)S(1)} %copy-done.3, bf16[896,4864]{1,0:T(8,128)(2,1)} %bitcast.298), kind=kOutput, calls=%fused_computation.207 | convolution fusion | flops 4462739456 | bytes 15532032 | tf_op jit(solution)/shard_map/dot_general | solution.py:63
  333.0 10.3 %multiply_reduce_fusion = (bf16[896]{0:T(1024)(128)(2,1)S(1)}, f32[512]{0:T(512)S(1)}, f32[512,896]{1,0:T(8,128)}) fusion(f32[512,896]{1,0:T(8,128)S(1)} %copy-done.8, f32[512]{0:T(512)S(1)} %add_rsqrt_fusion, f32[896]{0:T(1024)S(1)} %reshape.514, f32[512,896]{1,0:T(8,128)S(1)} %fusion.80, bf16[512,4864]{1,0:T(8,128)(2,1)S(1)} %bitcast.276, ...), kind=kOutput, calls=%fused_computation.81 | convolution fusion | flops 4465949184 | bytes 19211520 | tf_op jit(solution)/shard_map/dot_general | solution.py:63
  346.6 11.0 %add_convert_fusion.1 = bf16[512,896]{1,0:T(8,128)(2,1)} fusion(f32[512,896]{1,0:T(8,128)S(1)} %copy-done.8, bf16[512,4864]{1,0:T(8,128)(2,1)} %get-tuple-element.81, bf16[4864,896]{1,0:T(8,128)(2,1)} %all-gather.8.cloned.1.call-done), kind=kOutput, calls=%fused_computation.84 | convolution fusion | flops 4463656960 | bytes 16449536 | tf_op jit(solution)/shard_map/dot_general | solution.py:226
  357.7 7.3 %convolution_convert_fusion.2 = bf16[896,4864]{1,0:T(8,128)(2,1)} fusion(bf16[512,896]{1,0:T(8,128)(2,1)S(1)} %copy-done.17, bf16[512,4864]{1,0:T(8,128)(2,1)S(1)} %bitcast.280, bf16[512,4864]{1,0:T(8,128)(2,1)S(1)} %bitcast.278, pred[]{:T(512)S(6)} %eq.43), kind=kOutput, calls=%fused_computation.26 | convolution fusion | flops 4469587968 | bytes 19595264 | tf_op jit(solution)/shard_map/dot_general | solution.py:57
  365.0 6.9 %fusion.14 = bf16[16,152,896]{2,1,0:T(8,128)(2,1)} fusion(bf16[16,152,896]{2,1,0:T(8,128)(2,1)} %collective-permute-done.4, bf16[16,2,152,896]{3,2,1,0:T(8,128)(2,1)} %bitcast.294, s32[]{:T(128)S(6)} %select_n.162), kind=kLoop, calls=%fused_computation.28 | loop fusion | flops 8716288 | bytes 13074436 | tf_op jit(solution)/shard_map/convert_element_type | solution.py:232
  376.0 11.7 %fusion.43 = f32[1024,2,64]{0,2,1:T(8,128)S(1)} fusion(bf16[512,2,7,64]{0,3,2,1:T(8,128)(2,1)S(1)} %bitcast.299, f32[2,7,512,1024]{2,3,1,0:T(8,128)} %get-tuple-element.103, f32[2,7,512]{2,1,0:T(8,128)S(1)} %log_add_fusion), kind=kOutput, calls=%fused_computation.93 | convolution fusion | flops 954204160 | bytes 30830592 | tf_op jit(solution)/shard_map/kgqj,qkgd->jkd/dot_general | solution.py:288
  401.0 7.1 %add_convert_fusion = bf16[896,4864]{1,0:T(8,128)(2,1)S(1)} fusion(bf16[896,4864]{1,0:T(8,128)(2,1)} %collective-permute-done.3, bf16[896,4864]{1,0:T(8,128)(2,1)} %convolution_convert_fusion.2), kind=kLoop, calls=%fused_computation.11 | loop fusion | flops 17432576 | bytes 26148864 | tf_op jit(solution)/shard_map/convert_element_type | solution.py:257
  414.2 19.2 %fusion = (f32[2,7,512]{2,1,0:T(8,128)}, f32[2,1024,512,7]{2,1,3,0:T(8,128)}) fusion(f32[2,7,512,1024]{2,3,1,0:T(8,128)} %get-tuple-element.103, f32[2,7,512]{2,1,0:T(8,128)} %copy-done.48, bf16[1024,2,64,1]{0,2,3,1:T(8,128)(2,1)S(1)} %bitcast.308, bf16[512,2,7,64]{0,3,2,1:T(8,128)(2,1)S(1)} %bitcast.300), kind=kOutput, calls=%fused_computation.2 | convolution fusion | flops 961537024 | bytes 59957248 | tf_op jit(solution)/shard_map/qkgd,jkd->kgqj/dot_general | solution.py:278
  436.8 12.6 %collective-permute-done.5 = bf16[2,2,2,152,896]{4,3,2,1,0:T(8,128)(2,1)} collective-permute-done((bf16[2,2,2,152,896]{4,3,2,1,0:T(8,128)(2,1)}, bf16[2,2,2,152,896]{4,3,2,1,0:T(8,128)(2,1)}, u32[]{:S(2)}, u32[]{:S(2)}) %collective-permute-start.5) | collective-permute-done | bytes 2179104 | tf_op jit(solution)/shard_map/ppermute | solution.py:86
  452.2 8.0 %collective-permute-done.7 = bf16[2,2,2,56,2432]{4,3,2,1,0:T(8,128)(2,1)} collective-permute-done((bf16[2,2,2,56,2432]{4,3,2,1,0:T(8,128)(2,1)}, bf16[2,2,2,56,2432]{4,3,2,1,0:T(8,128)(2,1)}, u32[]{:S(2)}, u32[]{:S(2)}) %collective-permute-start.7) | collective-permute-done | bytes 2179104 | tf_op jit(solution)/shard_map/ppermute | solution.py:86
  467.3 25.3 %fusion.2 = bf16[2,7,512,1024]{2,3,1,0:T(8,128)(2,1)} fusion(f32[2,1024,512,7]{2,1,3,0:T(8,128)} %get-tuple-element.108, f32[2,7,512,1024]{2,3,1,0:T(8,128)} %get-tuple-element.103, f32[2,7,512]{2,1,0:T(8,128)S(1)} %copy-done.50, f32[2,7,512]{2,1,0:T(8,128)S(1)} %copy-done.49), kind=kLoop, calls=%fused_computation.4 | loop fusion | flops 29360128 | bytes 73457664 | tf_op jit(solution)/shard_map/convert_element_type | solution.py:283
  492.6 9.7 %fusion.47 = f32[1024,2,64]{0,2,1:T(8,128)S(1)} fusion(bf16[512,2,7,64]{0,3,2,1:T(8,128)(2,1)S(1)} %copy-done.1, bf16[2,7,512,1024]{2,3,1,0:T(8,128)(2,1)} %fusion.2), kind=kOutput, calls=%fused_computation.96 | convolution fusion | flops 939655168 | bytes 16121856 | tf_op jit(solution)/shard_map/kgqj,qkgd->jkd/dot_general | solution.py:285
  502.4 7.9 %convolution_multiply_fusion = f32[2,64,7,512]{3,1,2,0:T(8,128)S(1)} fusion(bf16[1024,2,64,1]{0,2,3,1:T(8,128)(2,1)S(1)} %bitcast.304, bf16[2,7,512,1024]{2,3,1,0:T(8,128)(2,1)} %fusion.2), kind=kOutput, calls=%fused_computation.88 | convolution fusion | flops 939982848 | bytes 16777216 | tf_op jit(solution)/shard_map/kgqj,jkd->qkgd/dot_general | solution.py:295
  526.0 15.8 %collective-permute-done.13 = bf16[2,2,56,2432]{3,2,1,0:T(8,128)(2,1)S(1)} collective-permute-done((bf16[2,2,56,2432]{3,2,1,0:T(8,128)(2,1)S(1)}, bf16[2,2,56,2432]{3,2,1,0:T(8,128)(2,1)S(1)}, u32[]{:S(2)}, u32[]{:S(2)}) %collective-permute-start.13) | collective-permute-done | bytes 1089568 | tf_op jit(solution)/shard_map/ppermute | solution.py:86
  543.0 5.4 collective-permute-done.12
  578.9 5.5 collective-permute-done.21
  601.4 24.4 %collective-permute-done.26 = bf16[56,2432]{1,0:T(8,128)(2,1)S(1)} collective-permute-done((bf16[56,2432]{1,0:T(8,128)(2,1)S(1)}, bf16[56,2432]{1,0:T(8,128)(2,1)S(1)}, u32[]{:S(2)}, u32[]{:S(2)}) %collective-permute-start.26) | collective-permute-done | bytes 272416 | tf_op jit(solution)/shard_map/ppermute | solution.py:86
  625.9 5.5 collective-permute-done.24
  635.2 13.4 %collective-permute-done.16 = bf16[2,2,2,29,1152]{4,2,3,1,0:T(2,128)(2,1)} collective-permute-done((bf16[2,2,2,29,1152]{4,2,3,1,0:T(2,128)(2,1)}, bf16[2,2,2,29,1152]{4,2,3,1,0:T(2,128)(2,1)}, u32[]{:S(2)}, u32[]{:S(2)}) %collective-permute-start.16) | collective-permute-done | bytes 534560 | tf_op jit(solution)/shard_map/ppermute | solution.py:86
  653.3 5.2 collective-permute-done.17
  (340 shorter events, 191.1 us)
Async XLA Ops:
  7.2 67.7 %all-gather.4.cloned.1.call-start = ((), (), s32[]{:S(2)}) async-start(), calls=%async_computation | async-start | bytes 3852288 | tf_op jit(solution)/shard_map/all_gather | solution.py:142
  11.0 187.5 %all-gather.6.cloned.1.call-start = ((), (), s32[]{:S(2)}) async-start(), calls=%async_computation.1 | async-start | bytes 17977344 | tf_op jit(solution)/shard_map/all_gather | solution.py:162
  80.0 198.7 %all-gather.8.cloned.1.call-start = ((), (), s32[]{:S(2)}) async-start(), calls=%async_computation.2 | async-start | bytes 8988672 | tf_op jit(solution)/shard_map/all_gather | solution.py:188
  103.0 13.8 %collective-permute-start = (bf16[512,128]{1,0:T(8,128)(2,1)}, bf16[512,128]{1,0:T(8,128)(2,1)}, u32[]{:S(2)}, u32[]{:S(2)}) collective-permute-start(bf16[512,128]{1,0:T(8,128)(2,1)} %slice.178), channel_id=1, source_target_pairs={{0,1},{1,2},{2,3},{3,4},{4,5},{5,6},{6,7},{7,8},{8,9},{9,10},{10,1... | collective-permute-start | bytes 393224 | tf_op jit(solution)/shard_map/ppermute | solution.py:23
  107.6 10.4 %collective-permute-start.1 = (bf16[512,128]{1,0:T(8,128)(2,1)}, bf16[512,128]{1,0:T(8,128)(2,1)}, u32[]{:S(2)}, u32[]{:S(2)}) collective-permute-start(bf16[512,128]{1,0:T(8,128)(2,1)} %add_convert_fusion.2), channel_id=1, source_target_pairs={{0,1},{1,2},{2,3},{3,4},{4,5},{5,6},{6,7},{7,8},{8,9},{9,10},{10,1... | collective-permute-start | bytes 393224 | tf_op jit(solution)/shard_map/ppermute | solution.py:23
  305.8 66.1 %collective-permute-start.3 = (bf16[896,4864]{1,0:T(8,128)(2,1)}, bf16[896,4864]{1,0:T(8,128)(2,1)}, u32[]{:S(2)}, u32[]{:S(2)}) collective-permute-start(bf16[896,4864]{1,0:T(8,128)(2,1)} %convolution_convert_fusion.1), channel_id=1, source_target_pairs={{0,1},{1,0},{2,3},{3,2},{4,5},{5,4},{6,7},{7,6},{8,9},{9,8},{10,11... | collective-permute-start | bytes 26148872 | tf_op jit(solution)/shard_map/ppermute | solution.py:86
  322.4 42.6 %collective-permute-start.4 = (bf16[16,152,896]{2,1,0:T(8,128)(2,1)}, bf16[16,152,896]{2,1,0:T(8,128)(2,1)}, u32[]{:S(2)}, u32[]{:S(2)}) collective-permute-start(bf16[16,152,896]{2,1,0:T(8,128)(2,1)} %dynamic-slice_bitcast_fusion), channel_id=1, source_target_pairs={{0,1},{1,0},{2,3},{3,2},{4,5},{5,4},{6,7},{7,6},{8,9},{9,8},{10,11... | collective-permute-start | bytes 13074440 | tf_op jit(solution)/shard_map/ppermute | solution.py:86
  388.4 45.0 %collective-permute-start.10 = (bf16[512,2,64]{0,2,1:T(8,128)(2,1)}, bf16[512,2,64]{0,2,1:T(8,128)(2,1)}, u32[]{:S(2)}, u32[]{:S(2)}) collective-permute-start(bf16[512,2,64]{0,2,1:T(8,128)(2,1)} %slice.176), channel_id=1, source_target_pairs={{1,0},{2,1},{3,2},{4,3},{5,4},{6,5},{7,6},{8,7},{9,8},{10,9},{11,1... | collective-permute-start | bytes 393224 | tf_op jit(solution)/shard_map/ppermute | solution.py:23
  394.1 40.2 %collective-permute-start.8 = (bf16[2,2,2,2,28,896]{5,3,4,2,1,0:T(2,128)(2,1)}, bf16[2,2,2,2,28,896]{5,3,4,2,1,0:T(2,128)(2,1)}, u32[]{:S(2)}, u32[]{:S(2)}) collective-permute-start(bf16[2,2,2,2,28,896]{5,3,4,2,1,0:T(2,128)(2,1)} %bitcast.269), channel_id=1, source_target_pairs={{0,1},{1,0},{2,3},{3,2},{4,5},{5,4},{6,7},{7,6},{8,9},{9,8},{10,11... | collective-permute-start | bytes 2408456 | tf_op jit(solution)/shard_map/ppermute | solution.py:86
  398.5 50.9 %collective-permute-start.5 = (bf16[2,2,2,152,896]{4,3,2,1,0:T(8,128)(2,1)}, bf16[2,2,2,152,896]{4,3,2,1,0:T(8,128)(2,1)}, u32[]{:S(2)}, u32[]{:S(2)}) collective-permute-start(bf16[2,2,2,152,896]{4,3,2,1,0:T(8,128)(2,1)} %dynamic-slice_bitcast_fusion.3), channel_id=1, source_target_pairs={{0,8},{1,9},{2,10},{3,11},{4,12},{5,13},{6,14},{7,15},{8,0},{9,1},... | collective-permute-start | bytes 6537224 | tf_op jit(solution)/shard_map/ppermute | solution.py:86
  410.4 49.8 %collective-permute-start.7 = (bf16[2,2,2,56,2432]{4,3,2,1,0:T(8,128)(2,1)}, bf16[2,2,2,56,2432]{4,3,2,1,0:T(8,128)(2,1)}, u32[]{:S(2)}, u32[]{:S(2)}) collective-permute-start(bf16[2,2,2,56,2432]{4,3,2,1,0:T(8,128)(2,1)} %dynamic-slice_bitcast_fusion.1), channel_id=1, source_target_pairs={{0,4},{1,5},{2,6},{3,7},{4,0},{5,1},{6,2},{7,3},{8,12},{9,13},{10,... | collective-permute-start | bytes 6537224 | tf_op jit(solution)/shard_map/ppermute | solution.py:86
  413.6 50.2 %collective-permute-start.6 = (bf16[2,2,2,56,2432]{4,3,2,1,0:T(8,128)(2,1)}, bf16[2,2,2,56,2432]{4,3,2,1,0:T(8,128)(2,1)}, u32[]{:S(2)}, u32[]{:S(2)}) collective-permute-start(bf16[2,2,2,56,2432]{4,3,2,1,0:T(8,128)(2,1)} %dynamic-slice_bitcast_fusion.2), channel_id=1, source_target_pairs={{0,2},{1,3},{2,0},{3,1},{4,6},{5,7},{6,4},{7,5},{8,10},{9,11},{10,... | collective-permute-start | bytes 6537224 | tf_op jit(solution)/shard_map/ppermute | solution.py:86
  510.3 9.7 %collective-permute-start.9 = (bf16[512,2,64]{0,2,1:T(8,128)(2,1)S(1)}, bf16[512,2,64]{0,2,1:T(8,128)(2,1)S(1)}, u32[]{:S(2)}, u32[]{:S(2)}) collective-permute-start(bf16[512,2,64]{0,2,1:T(8,128)(2,1)S(1)} %slice.177), channel_id=1, source_target_pairs={{1,0},{2,1},{3,2},{4,3},{5,4},{6,5},{7,6},{8,7},{9,8},{10,9},{11,1... | collective-permute-start | bytes 393224 | tf_op jit(solution)/shard_map/ppermute | solution.py:23
  511.8 13.3 %collective-permute-start.14 = (bf16[2,2,2,28,896]{4,3,2,1,0:T(8,128)(2,1)S(1)}, bf16[2,2,2,28,896]{4,3,2,1,0:T(8,128)(2,1)S(1)}, u32[]{:S(2)}, u32[]{:S(2)}) collective-permute-start(bf16[2,2,2,28,896]{4,3,2,1,0:T(8,128)(2,1)S(1)} %dynamic-slice_bitcast_fusion.11), channel_id=1, source_target_pairs={{0,4},{1,5},{2,6},{3,7},{4,0},{5,1},{6,2},{7,3},{8,12},{9,13},{10,... | collective-permute-start | bytes 1204232 | tf_op jit(solution)/shard_map/ppermute | solution.py:86
  515.5 26.2 %collective-permute-start.13 = (bf16[2,2,56,2432]{3,2,1,0:T(8,128)(2,1)S(1)}, bf16[2,2,56,2432]{3,2,1,0:T(8,128)(2,1)S(1)}, u32[]{:S(2)}, u32[]{:S(2)}) collective-permute-start(bf16[2,2,56,2432]{3,2,1,0:T(8,128)(2,1)S(1)} %dynamic-slice_bitcast_fusion.4), channel_id=1, source_target_pairs={{0,8},{1,9},{2,10},{3,11},{4,12},{5,13},{6,14},{7,15},{8,0},{9,1},... | collective-permute-start | bytes 3268616 | tf_op jit(solution)/shard_map/ppermute | solution.py:86
  516.3 32.1 %collective-permute-start.12 = (bf16[2,2,56,2432]{3,2,1,0:T(8,128)(2,1)S(1)}, bf16[2,2,56,2432]{3,2,1,0:T(8,128)(2,1)S(1)}, u32[]{:S(2)}, u32[]{:S(2)}) collective-permute-start(bf16[2,2,56,2432]{3,2,1,0:T(8,128)(2,1)S(1)} %dynamic-slice_bitcast_fusion.5), channel_id=1, source_target_pairs={{0,4},{1,5},{2,6},{3,7},{4,0},{5,1},{6,2},{7,3},{8,12},{9,13},{10,... | collective-permute-start | bytes 3268616 | tf_op jit(solution)/shard_map/ppermute | solution.py:86
  518.3 31.5 %collective-permute-start.11 = (bf16[2,2,152,896]{3,2,1,0:T(8,128)(2,1)S(1)}, bf16[2,2,152,896]{3,2,1,0:T(8,128)(2,1)S(1)}, u32[]{:S(2)}, u32[]{:S(2)}) collective-permute-start(bf16[2,2,152,896]{3,2,1,0:T(8,128)(2,1)S(1)} %dynamic-slice_bitcast_fusion.6), channel_id=1, source_target_pairs={{0,2},{1,3},{2,0},{3,1},{4,6},{5,7},{6,4},{7,5},{8,10},{9,11},{10,... | collective-permute-start | bytes 3268616 | tf_op jit(solution)/shard_map/ppermute | solution.py:86
  563.5 11.1 %collective-permute-start.20 = (bf16[2,2,28,896]{3,2,1,0:T(8,128)(2,1)}, bf16[2,2,28,896]{3,2,1,0:T(8,128)(2,1)}, u32[]{:S(2)}, u32[]{:S(2)}) collective-permute-start(bf16[2,2,28,896]{3,2,1,0:T(8,128)(2,1)} %dynamic-slice_bitcast_fusion.16), channel_id=1, source_target_pairs={{0,8},{1,9},{2,10},{3,11},{4,12},{5,13},{6,14},{7,15},{8,0},{9,1},... | collective-permute-start | bytes 602120 | tf_op jit(solution)/shard_map/ppermute | solution.py:86
  566.6 25.8 %collective-permute-start.28 = (bf16[2,152,896]{2,1,0:T(8,128)(2,1)}, bf16[2,152,896]{2,1,0:T(8,128)(2,1)}, u32[]{:S(2)}, u32[]{:S(2)}) collective-permute-start(bf16[2,152,896]{2,1,0:T(8,128)(2,1)} %dynamic-slice_bitcast_fusion.8), channel_id=1, source_target_pairs={{0,4},{1,5},{2,6},{3,7},{4,0},{5,1},{6,2},{7,3},{8,12},{9,13},{10,... | collective-permute-start | bytes 1634312 | tf_op jit(solution)/shard_map/ppermute | solution.py:86
  568.2 27.7 %collective-permute-start.25 = (bf16[2,56,2432]{2,1,0:T(8,128)(2,1)}, bf16[2,56,2432]{2,1,0:T(8,128)(2,1)}, u32[]{:S(2)}, u32[]{:S(2)}) collective-permute-start(bf16[2,56,2432]{2,1,0:T(8,128)(2,1)} %dynamic-slice_bitcast_fusion.9), channel_id=1, source_target_pairs={{0,2},{1,3},{2,0},{3,1},{4,6},{5,7},{6,4},{7,5},{8,10},{9,11},{10,... | collective-permute-start | bytes 1634312 | tf_op jit(solution)/shard_map/ppermute | solution.py:86
  570.4 28.5 %collective-permute-start.23 = (bf16[2,56,2432]{2,1,0:T(8,128)(2,1)}, bf16[2,56,2432]{2,1,0:T(8,128)(2,1)}, u32[]{:S(2)}, u32[]{:S(2)}) collective-permute-start(bf16[2,56,2432]{2,1,0:T(8,128)(2,1)} %dynamic-slice_bitcast_fusion.10), channel_id=1, source_target_pairs={{0,8},{1,9},{2,10},{3,11},{4,12},{5,13},{6,14},{7,15},{8,0},{9,1},... | collective-permute-start | bytes 1634312 | tf_op jit(solution)/shard_map/ppermute | solution.py:86
  575.7 8.7 %collective-permute-start.21 = (bf16[2,28,896]{2,1,0:T(8,128)(2,1)S(1)}, bf16[2,28,896]{2,1,0:T(8,128)(2,1)S(1)}, u32[]{:S(2)}, u32[]{:S(2)}) collective-permute-start(bf16[2,28,896]{2,1,0:T(8,128)(2,1)S(1)} %dynamic-slice_bitcast_fusion.18), channel_id=1, source_target_pairs={{0,2},{1,3},{2,0},{3,1},{4,6},{5,7},{6,4},{7,5},{8,10},{9,11},{10,... | collective-permute-start | bytes 301064 | tf_op jit(solution)/shard_map/ppermute | solution.py:86
  578.9 52.5 %collective-permute-start.15 = (bf16[2,2,2,2,29,1152]{5,3,4,2,1,0:T(2,128)(2,1)}, bf16[2,2,2,2,29,1152]{5,3,4,2,1,0:T(2,128)(2,1)}, u32[]{:S(2)}, u32[]{:S(2)}) collective-permute-start(bf16[2,2,2,2,29,1152]{5,3,4,2,1,0:T(2,128)(2,1)} %bitcast.268), channel_id=1, source_target_pairs={{0,1},{1,0},{2,3},{3,2},{4,5},{5,4},{6,7},{7,6},{8,9},{9,8},{10,11... | collective-permute-start | bytes 3207176 | tf_op jit(solution)/shard_map/ppermute | solution.py:86
  584.5 5.6 collective-permute-start.22
  594.6 56.9 %collective-permute-start.29 = (bf16[152,896]{1,0:T(8,128)(2,1)}, bf16[152,896]{1,0:T(8,128)(2,1)}, u32[]{:S(2)}, u32[]{:S(2)}) collective-permute-start(bf16[152,896]{1,0:T(8,128)(2,1)} %dynamic-slice_bitcast_fusion.13), channel_id=1, source_target_pairs={{0,16},{1,17},{2,18},{3,19},{4,20},{5,21},{6,22},{7,23},{8,24},{9,... | collective-permute-start | bytes 817160 | tf_op jit(solution)/shard_map/ppermute | solution.py:86
  597.1 28.7 %collective-permute-start.26 = (bf16[56,2432]{1,0:T(8,128)(2,1)S(1)}, bf16[56,2432]{1,0:T(8,128)(2,1)S(1)}, u32[]{:S(2)}, u32[]{:S(2)}) collective-permute-start(bf16[56,2432]{1,0:T(8,128)(2,1)S(1)} %dynamic-slice_bitcast_fusion.14), channel_id=1, source_target_pairs={{0,16},{1,17},{2,18},{3,19},{4,20},{5,21},{6,22},{7,23},{8,24},{9,... | collective-permute-start | bytes 817160 | tf_op jit(solution)/shard_map/ppermute | solution.py:86
  600.1 31.3 %collective-permute-start.24 = (bf16[56,2432]{1,0:T(8,128)(2,1)S(1)}, bf16[56,2432]{1,0:T(8,128)(2,1)S(1)}, u32[]{:S(2)}, u32[]{:S(2)}) collective-permute-start(bf16[56,2432]{1,0:T(8,128)(2,1)S(1)} %dynamic-slice_bitcast_fusion.15), channel_id=1, source_target_pairs={{0,16},{1,17},{2,18},{3,19},{4,20},{5,21},{6,22},{7,23},{8,24},{9,... | collective-permute-start | bytes 817160 | tf_op jit(solution)/shard_map/ppermute | solution.py:86
  634.4 14.2 %collective-permute-start.16 = (bf16[2,2,2,29,1152]{4,2,3,1,0:T(2,128)(2,1)}, bf16[2,2,2,29,1152]{4,2,3,1,0:T(2,128)(2,1)}, u32[]{:S(2)}, u32[]{:S(2)}) collective-permute-start(bf16[2,2,2,29,1152]{4,2,3,1,0:T(2,128)(2,1)} %bitcast.270), channel_id=1, source_target_pairs={{0,2},{1,3},{2,0},{3,1},{4,6},{5,7},{6,4},{7,5},{8,10},{9,11},{10,... | collective-permute-start | bytes 1603592 | tf_op jit(solution)/shard_map/ppermute | solution.py:86
  650.5 8.1 %collective-permute-start.17 = (bf16[2,2,29,1152]{3,2,1,0:T(8,128)(2,1)}, bf16[2,2,29,1152]{3,2,1,0:T(8,128)(2,1)S(1)}, u32[]{:S(2)}, u32[]{:S(2)}) collective-permute-start(bf16[2,2,29,1152]{3,2,1,0:T(8,128)(2,1)} %dynamic-slice_bitcast_fusion.12), channel_id=1, source_target_pairs={{0,4},{1,5},{2,6},{3,7},{4,0},{5,1},{6,2},{7,3},{8,12},{9,13},{10,... | collective-permute-start | bytes 801800 | tf_op jit(solution)/shard_map/ppermute | solution.py:86
  653.3 5.4 collective-permute-start.27
  658.7 5.2 collective-permute-start.18
  664.0 5.7 collective-permute-start.19
  (70 other events, 838.2 us)
Sparse Core Ops, SparseCore 0:
  11.5 63.2 all-gather.3
  80.2 118.2 all-gather.5
  202.0 76.7 all-gather.7

commit v3 on v2

--- a/solution.py
+++ b/solution.py
@@ -110,7 +110,7 @@
 
 
 def reduce_to_owner(x, bits, order):
-    return reduce_step(x, bits, order, len(order))[0]
+    return reduce_step(x, bits, order, len(order))[0] if order else x
 
 
 def norm_back(grad_normed, hidden, factor, gain):
@@ -281,6 +281,7 @@
     inner = jnp.sum(probs * grad_probs, axis=-1, keepdims=True)
     moving, inner = one_step(moving, inner)
     grad_scores = (probs * (grad_probs - inner)).astype(jnp.bfloat16)
+    moving, grad_scores = one_step(moving, grad_scores)
     grad_key = (
         jnp.einsum("kgqj,qkgd->jkd", grad_scores, rows_q, preferred_element_type=jnp.float32)
         * scale
@@ -326,7 +327,9 @@
     else:
         grad_wqkv = grad_wqkv.reshape(n_devices, -1)
     last = jnp.concatenate([grad_wqkv, vectors], axis=1).astype(jnp.bfloat16)
-    last_sum = reduce_to_owner(last, bits, (0, 1, 2, 3) + far).reshape(-1)
+    last, last_bits, last_order = reduce_step(last, bits, (0, 1, 2, 3) + far, 3)
+    moving, last = one_step(moving, last)
+    last_sum = reduce_to_owner(last, last_bits, last_order).reshape(-1)
     qkv_own = w_qkv.shape[0]
     sums = [reduce_to_owner(*part) for part in moving]
     down_sum, wout_sum = sums[0], sums[-1]

time: 686 us -> 626 us (0.913)
  waiting for transfers between devices: 263 us -> 213 us
  other arithmetic: 100 us -> 92.6 us
    ppermute x26, waiting for transfers between devices: 110 us -> 60.6 us  [partner_swap(): return lax.ppermute(x, 'fsdp', [(i, i ^ 1 << bit) for i in range(peers)])]
  transfers between devices with their start and end apart: 33 -> 33, of which waited for: 16 -> 17; matrix products, arithmetic and copies ran while one was open for 35% -> 41% of each run, Pallas kernels for 0% -> 0%
where the time goes in v3:
time: 626 us; the launch traced here: 618 us
  waiting for transfers between devices  213 us (34%)
  matrix products  180 us (29%)
  other arithmetic  92.6 us (15%)
  local copies, waits for them, and re-layouts  78 us (12%)
  starting transfers between devices  38.7 us (6%)
  between operations  15.4 us (2%)
    ppermute x26, waiting for transfers between devices, partner_swap(): return lax.ppermute(x, 'fsdp', [(i, i ^ 1 << bit) for i in range(peers)])  60.6 us
    all_gather x1, waiting for transfers between devices, local(): lax.all_gather(attn_flat, 'fsdp', axis=0, tiled=True).reshape(n_devices, -1)  57.9 us
    all_gather x1, waiting for transfers between devices, local(): wdown = lax.all_gather(down_own, 'fsdp', axis=0, tiled=True)  56.2 us
    dot_general x5, matrix products, back_dot(): lax.dot_general(left, right, (((1,), (1,)), ((), ())), preferred_element_...  42.5 us
    all_gather x1, waiting for transfers between devices, local(): gu_all = lax.all_gather(gu_chip, 'fsdp', axis=0, tiled=True)  38.3 us
    dot_general x5, matrix products, outer_sum(): lax.dot_general(left, right, (((0,), (0,)), ((), ())), preferred_element_...  30.4 us
    ppermute x26, starting transfers between devices, partner_swap(): return lax.ppermute(x, 'fsdp', [(i, i ^ 1 << bit) for i in range(peers)])  29.9 us
    convert_element_type x1, other arithmetic, local(): grad_scores = (probs * (grad_probs - inner)).astype(jnp.bfloat16)  25.3 us
  transfers between devices with their start and end apart: 33, of which 17 were waited for; matrix products, arithmetic and copies ran while one was open for 41% of the time, Pallas kernels for 0%

profile of v3, /device:TPU:0, one launch (start us, length us, event | category | flops | bytes accessed | tf_op | source)
XLA Modules:
  0.0 618.0 jit_solution(7904865495319346055)
XLA Ops:
  16.9 57.9 %all-gather.4.cloned.1.call-done = bf16[1867776]{0:T(1024)(128)(2,1)} async-done(((bf16[58368]{0:T(1024)(128)(2,1)}), bf16[1867776]{0:T(1024)(128)(2,1)}) %all-gather.4.cloned.1.call-update) | async-done | bytes 3735568 | tf_op jit(solution)/shard_map/all_gather | solution.py:142
  74.8 5.2 reshape.481
  89.0 4.2 reshape_reshape.9
  119.2 12.0 %fusion.77 = (f32[2,7,512]{2,1,0:T(8,128)S(1)}, f32[2,7,512,1024]{2,3,1,0:T(8,128)}) fusion(bf16[1024,2,64,1]{0,2,3,1:T(8,128)(2,1)S(1)} %bitcast.307, bf16[512,2,7,64]{0,3,2,1:T(8,128)(2,1)S(1)} %fusion.38, pred[512,1024]{0,1:T(8,128)(4,1)S(1)} %and_and_fusion), kind=kOutput, calls=%fused_computation.204 | convolution fusion | flops 961537024 | bytes 31092736 | tf_op jit(solution)/shard_map/while/body/eval_jaxpr/qkgd,jkd->kgqj/dot_general | solution.py:201
  131.2 11.7 %fusion.3 = f32[2,7,512]{2,1,0:T(8,128)S(1)} fusion(f32[2,7,512,1024]{2,3,1,0:T(8,128)} %get-tuple-element.123, f32[2,7,512]{2,1,0:T(8,128)S(1)} %get-tuple-element.122), kind=kLoop, calls=%fused_computation.9 | loop fusion | flops 14672896 | bytes 29417472 | tf_op jit(solution)/shard_map/while/body/eval_jaxpr/reduce_sum | solution.py:211
  142.9 14.3 %fusion.42 = bf16[2,64,7,512]{3,1,2,0:T(8,128)(2,1)S(1)} fusion(bf16[1024,2,64,1]{0,2,3,1:T(8,128)(2,1)S(1)} %bitcast.312, f32[2,7,512,1024]{2,3,1,0:T(8,128)} %get-tuple-element.123, f32[2,7,512]{2,1,0:T(8,128)S(1)} %fusion.3, f32[2,7,512]{2,1,0:T(8,128)S(1)} %get-tuple-element.122), kind=kOutput, calls=%fused_computation.91 | convolution fusion | flops 962002944 | bytes 30597120 | tf_op jit(solution)/shard_map/while/body/eval_jaxpr/kgqj,jkd->qkgd/dot_general | solution.py:213
  160.2 38.3 %all-gather.6.cloned.1.call-done = bf16[1792,4864]{1,0:T(8,128)(2,1)} async-done(((bf16[56,4864]{1,0:T(8,128)(2,1)}), bf16[1792,4864]{1,0:T(8,128)(2,1)}) %all-gather.6.cloned.1.call-update) | async-done | bytes 17432592 | tf_op jit(solution)/shard_map/all_gather | solution.py:162
  198.5 6.6 %fusion.75 = (bf16[16,1,56,4864]{3,2,1,0:T(8,128)(2,1)S(1)}, bf16[16,1,56,4864]{3,2,1,0:T(8,128)(2,1)S(1)}) fusion(bf16[16,2,56,4864]{3,2,1,0:T(8,128)(2,1)} %bitcast.285), kind=kLoop, calls=%fused_computation.202 | loop fusion | bytes 34865152 | tf_op jit(solution)/shard_map/slice | solution.py:164
  205.1 8.6 %fusion.79 = f32[512,4864]{1,0:T(8,128)} fusion(bf16[512,896]{1,0:T(8,128)(2,1)S(1)} %multiply_convert_fusion.1, bf16[896,4864]{1,0:T(8,128)(2,1)S(1)} %bitcast.299), kind=kOutput, calls=%fused_computation.206 | convolution fusion | flops 4462739456 | bytes 19595264 | tf_op jit(solution)/shard_map/dot_general | solution.py:222
  214.3 8.2 %fusion.78 = f32[512,4864]{1,0:T(8,128)} fusion(bf16[512,896]{1,0:T(8,128)(2,1)S(1)} %multiply_convert_fusion.1, bf16[896,4864]{1,0:T(8,128)(2,1)S(1)} %bitcast.301), kind=kOutput, calls=%fused_computation.205 | convolution fusion | flops 4462739456 | bytes 19595264 | tf_op jit(solution)/shard_map/dot_general | solution.py:221
  222.6 56.2 %all-gather.8.cloned.1.call-done = bf16[4864,896]{1,0:T(8,128)(2,1)} async-done(((bf16[152,896]{1,0:T(8,128)(2,1)}), bf16[4864,896]{1,0:T(8,128)(2,1)}) %all-gather.8.cloned.1.call-update) | async-done | bytes 8716304 | tf_op jit(solution)/shard_map/all_gather | solution.py:188
  278.8 16.8 %fusion.12 = (bf16[512,4864]{1,0:T(8,128)(2,1)S(1)}, bf16[512,4864]{1,0:T(8,128)(2,1)}, bf16[512,4864]{1,0:T(8,128)(2,1)}) fusion(f32[512,4864]{1,0:T(8,128)} %fusion.78, f32[512,4864]{1,0:T(8,128)} %fusion.79, bf16[4864,896]{1,0:T(8,128)(2,1)} %all-gather.8.cloned.1.call-done, bf16[512,896]{1,0:T(8,128)(2,1)} %param.17), kind=kOutput, calls=%fused_computation.20 | convolution fusion | flops 4500094976 | bytes 44498944 | tf_op jit(solution)/shard_map/dot_general | solution.py:63
  295.6 10.1 %convolution_convert_fusion.1 = bf16[896,4864]{1,0:T(8,128)(2,1)} fusion(bf16[512,896]{1,0:T(8,128)(2,1)} %copy-done.17, bf16[512,4864]{1,0:T(8,128)(2,1)S(1)} %get-tuple-element.99, bf16[512,4864]{1,0:T(8,128)(2,1)} %get-tuple-element.100, pred[]{:T(512)S(6)} %eq.43), kind=kOutput, calls=%fused_computation.25 | convolution fusion | flops 4469587968 | bytes 19595264 | tf_op jit(solution)/shard_map/dot_general | solution.py:57
  308.6 7.9 %convolution_convert_fusion = bf16[4864,896]{1,0:T(8,128)(2,1)S(1)} fusion(bf16[512,4864]{1,0:T(8,128)(2,1)} %get-tuple-element.101, bf16[512,896]{1,0:T(8,128)(2,1)} %param.17), kind=kOutput, calls=%fused_computation.24 | convolution fusion | flops 4467097600 | bytes 14614528 | tf_op jit(solution)/shard_map/dot_general | solution.py:57
  322.2 10.5 %fusion.80 = f32[512,896]{1,0:T(8,128)S(1)} fusion(bf16[512,4864]{1,0:T(8,128)(2,1)S(1)} %copy-done.3, bf16[896,4864]{1,0:T(8,128)(2,1)} %bitcast.302), kind=kOutput, calls=%fused_computation.207 | convolution fusion | flops 4462739456 | bytes 15532032 | tf_op jit(solution)/shard_map/dot_general | solution.py:63
  332.8 10.4 %multiply_reduce_fusion = (bf16[896]{0:T(1024)(128)(2,1)S(1)}, f32[512]{0:T(512)S(1)}, f32[512,896]{1,0:T(8,128)}) fusion(f32[512,896]{1,0:T(8,128)S(1)} %copy-done.8, f32[512]{0:T(512)S(1)} %add_rsqrt_fusion, f32[896]{0:T(1024)S(1)} %reshape.530, f32[512,896]{1,0:T(8,128)S(1)} %fusion.80, bf16[512,4864]{1,0:T(8,128)(2,1)S(1)} %bitcast.280, ...), kind=kOutput, calls=%fused_computation.81 | convolution fusion | flops 4465949184 | bytes 19211520 | tf_op jit(solution)/shard_map/dot_general | solution.py:63
  347.1 11.0 %add_convert_fusion.1 = bf16[512,896]{1,0:T(8,128)(2,1)} fusion(f32[512,896]{1,0:T(8,128)S(1)} %copy-done.8, bf16[512,4864]{1,0:T(8,128)(2,1)} %get-tuple-element.101, bf16[4864,896]{1,0:T(8,128)(2,1)} %all-gather.8.cloned.1.call-done), kind=kOutput, calls=%fused_computation.84 | convolution fusion | flops 4463656960 | bytes 16449536 | tf_op jit(solution)/shard_map/dot_general | solution.py:226
  358.1 7.3 %convolution_convert_fusion.2 = bf16[896,4864]{1,0:T(8,128)(2,1)} fusion(bf16[512,896]{1,0:T(8,128)(2,1)S(1)} %copy-done.18, bf16[512,4864]{1,0:T(8,128)(2,1)S(1)} %bitcast.284, bf16[512,4864]{1,0:T(8,128)(2,1)S(1)} %bitcast.282, pred[]{:T(512)S(6)} %eq.43), kind=kOutput, calls=%fused_computation.26 | convolution fusion | flops 4469587968 | bytes 19595264 | tf_op jit(solution)/shard_map/dot_general | solution.py:57
  365.4 6.9 %fusion.14 = bf16[16,152,896]{2,1,0:T(8,128)(2,1)} fusion(bf16[16,152,896]{2,1,0:T(8,128)(2,1)} %collective-permute-done.4, bf16[16,2,152,896]{3,2,1,0:T(8,128)(2,1)} %bitcast.298, s32[]{:T(128)S(6)} %select_n.162), kind=kLoop, calls=%fused_computation.28 | loop fusion | flops 8716288 | bytes 13074436 | tf_op jit(solution)/shard_map/convert_element_type | solution.py:232
  376.4 11.7 %fusion.43 = f32[1024,2,64]{0,2,1:T(8,128)S(1)} fusion(bf16[512,2,7,64]{0,3,2,1:T(8,128)(2,1)S(1)} %bitcast.303, f32[2,7,512,1024]{2,3,1,0:T(8,128)} %get-tuple-element.123, f32[2,7,512]{2,1,0:T(8,128)S(1)} %log_add_fusion), kind=kOutput, calls=%fused_computation.93 | convolution fusion | flops 954204160 | bytes 30830592 | tf_op jit(solution)/shard_map/kgqj,qkgd->jkd/dot_general | solution.py:289
  401.5 7.1 %add_convert_fusion = bf16[896,4864]{1,0:T(8,128)(2,1)S(1)} fusion(bf16[896,4864]{1,0:T(8,128)(2,1)} %collective-permute-done.3, bf16[896,4864]{1,0:T(8,128)(2,1)} %convolution_convert_fusion.2), kind=kLoop, calls=%fused_computation.11 | loop fusion | flops 17432576 | bytes 26148864 | tf_op jit(solution)/shard_map/convert_element_type | solution.py:257
  414.6 19.2 %fusion = (f32[2,7,512]{2,1,0:T(8,128)}, f32[2,1024,512,7]{2,1,3,0:T(8,128)}) fusion(f32[2,7,512,1024]{2,3,1,0:T(8,128)} %get-tuple-element.123, f32[2,7,512]{2,1,0:T(8,128)} %copy-done.47, bf16[1024,2,64,1]{0,2,3,1:T(8,128)(2,1)S(1)} %bitcast.313, bf16[512,2,7,64]{0,3,2,1:T(8,128)(2,1)S(1)} %bitcast.304), kind=kOutput, calls=%fused_computation.2 | convolution fusion | flops 961537024 | bytes 59957248 | tf_op jit(solution)/shard_map/qkgd,jkd->kgqj/dot_general | solution.py:278
  436.3 13.5 %collective-permute-done.5 = bf16[2,2,2,152,896]{4,3,2,1,0:T(8,128)(2,1)} collective-permute-done((bf16[2,2,2,152,896]{4,3,2,1,0:T(8,128)(2,1)}, bf16[2,2,2,152,896]{4,3,2,1,0:T(8,128)(2,1)}, u32[]{:S(2)}, u32[]{:S(2)}) %collective-permute-start.5) | collective-permute-done | bytes 2179104 | tf_op jit(solution)/shard_map/ppermute | solution.py:86
  452.7 8.0 %collective-permute-done.7 = bf16[2,2,2,56,2432]{4,3,2,1,0:T(8,128)(2,1)} collective-permute-done((bf16[2,2,2,56,2432]{4,3,2,1,0:T(8,128)(2,1)}, bf16[2,2,2,56,2432]{4,3,2,1,0:T(8,128)(2,1)}, u32[]{:S(2)}, u32[]{:S(2)}) %collective-permute-start.7) | collective-permute-done | bytes 2179104 | tf_op jit(solution)/shard_map/ppermute | solution.py:86
  473.3 25.3 %fusion.2 = bf16[2,7,512,1024]{2,3,1,0:T(8,128)(2,1)} fusion(f32[2,1024,512,7]{2,1,3,0:T(8,128)} %get-tuple-element.128, f32[2,7,512,1024]{2,3,1,0:T(8,128)} %get-tuple-element.123, f32[2,7,512]{2,1,0:T(8,128)S(1)} %copy-done.49, f32[2,7,512]{2,1,0:T(8,128)S(1)} %copy-done.48), kind=kLoop, calls=%fused_computation.4 | loop fusion | flops 29360128 | bytes 73457664 | tf_op jit(solution)/shard_map/convert_element_type | solution.py:283
  505.6 9.7 %fusion.47 = f32[1024,2,64]{0,2,1:T(8,128)S(1)} fusion(bf16[512,2,7,64]{0,3,2,1:T(8,128)(2,1)S(1)} %copy-done.1, bf16[2,7,512,1024]{2,3,1,0:T(8,128)(2,1)} %fusion.2), kind=kOutput, calls=%fused_computation.96 | convolution fusion | flops 939655168 | bytes 16121856 | tf_op jit(solution)/shard_map/kgqj,qkgd->jkd/dot_general | solution.py:286
  515.3 7.8 %convolution_multiply_fusion = f32[2,64,7,512]{3,1,2,0:T(8,128)S(1)} fusion(bf16[1024,2,64,1]{0,2,3,1:T(8,128)(2,1)S(1)} %bitcast.308, bf16[2,7,512,1024]{2,3,1,0:T(8,128)(2,1)} %fusion.2), kind=kOutput, calls=%fused_computation.88 | convolution fusion | flops 939982848 | bytes 16777216 | tf_op jit(solution)/shard_map/kgqj,jkd->qkgd/dot_general | solution.py:296
  535.7 6.3 %collective-permute-done.15 = bf16[2,152,896]{2,1,0:T(8,128)(2,1)S(1)} collective-permute-done((bf16[2,152,896]{2,1,0:T(8,128)(2,1)S(1)}, bf16[2,152,896]{2,1,0:T(8,128)(2,1)S(1)}, u32[]{:S(2)}, u32[]{:S(2)}) %collective-permute-start.15) | collective-permute-done | bytes 544800 | tf_op jit(solution)/shard_map/ppermute | solution.py:86
  545.9 3.6 fusion.35
  564.9 3.8 fusion.33
  572.0 11.2 %collective-permute-done.24 = bf16[56,2432]{1,0:T(8,128)(2,1)} collective-permute-done((bf16[56,2432]{1,0:T(8,128)(2,1)}, bf16[56,2432]{1,0:T(8,128)(2,1)}, u32[]{:S(2)}, u32[]{:S(2)}) %collective-permute-start.24) | collective-permute-done | bytes 272416 | tf_op jit(solution)/shard_map/ppermute | solution.py:86
  594.4 3.6 collective-permute-start.26
  (344 shorter events, 167.6 us)
Async XLA Ops:
  7.2 67.7 %all-gather.4.cloned.1.call-start = ((), (), s32[]{:S(2)}) async-start(), calls=%async_computation | async-start | bytes 3852288 | tf_op jit(solution)/shard_map/all_gather | solution.py:142
  11.0 187.4 %all-gather.6.cloned.1.call-start = ((), (), s32[]{:S(2)}) async-start(), calls=%async_computation.1 | async-start | bytes 17977344 | tf_op jit(solution)/shard_map/all_gather | solution.py:162
  80.0 198.7 %all-gather.8.cloned.1.call-start = ((), (), s32[]{:S(2)}) async-start(), calls=%async_computation.2 | async-start | bytes 8988672 | tf_op jit(solution)/shard_map/all_gather | solution.py:188
  103.0 13.8 %collective-permute-start = (bf16[512,128]{1,0:T(8,128)(2,1)}, bf16[512,128]{1,0:T(8,128)(2,1)}, u32[]{:S(2)}, u32[]{:S(2)}) collective-permute-start(bf16[512,128]{1,0:T(8,128)(2,1)} %slice.178), channel_id=1, source_target_pairs={{0,1},{1,2},{2,3},{3,4},{4,5},{5,6},{6,7},{7,8},{8,9},{9,10},{10,1... | collective-permute-start | bytes 393224 | tf_op jit(solution)/shard_map/ppermute | solution.py:23
  107.6 10.4 %collective-permute-start.1 = (bf16[512,128]{1,0:T(8,128)(2,1)}, bf16[512,128]{1,0:T(8,128)(2,1)}, u32[]{:S(2)}, u32[]{:S(2)}) collective-permute-start(bf16[512,128]{1,0:T(8,128)(2,1)} %add_convert_fusion.2), channel_id=1, source_target_pairs={{0,1},{1,2},{2,3},{3,4},{4,5},{5,6},{6,7},{7,8},{8,9},{9,10},{10,1... | collective-permute-start | bytes 393224 | tf_op jit(solution)/shard_map/ppermute | solution.py:23
  305.7 66.7 %collective-permute-start.3 = (bf16[896,4864]{1,0:T(8,128)(2,1)}, bf16[896,4864]{1,0:T(8,128)(2,1)}, u32[]{:S(2)}, u32[]{:S(2)}) collective-permute-start(bf16[896,4864]{1,0:T(8,128)(2,1)} %convolution_convert_fusion.1), channel_id=1, source_target_pairs={{0,1},{1,0},{2,3},{3,2},{4,5},{5,4},{6,7},{7,6},{8,9},{9,8},{10,11... | collective-permute-start | bytes 26148872 | tf_op jit(solution)/shard_map/ppermute | solution.py:86
  322.2 43.2 %collective-permute-start.4 = (bf16[16,152,896]{2,1,0:T(8,128)(2,1)}, bf16[16,152,896]{2,1,0:T(8,128)(2,1)}, u32[]{:S(2)}, u32[]{:S(2)}) collective-permute-start(bf16[16,152,896]{2,1,0:T(8,128)(2,1)} %dynamic-slice_bitcast_fusion), channel_id=1, source_target_pairs={{0,1},{1,0},{2,3},{3,2},{4,5},{5,4},{6,7},{7,6},{8,9},{9,8},{10,11... | collective-permute-start | bytes 13074440 | tf_op jit(solution)/shard_map/ppermute | solution.py:86
  388.8 45.0 %collective-permute-start.14 = (bf16[512,2,64]{0,2,1:T(8,128)(2,1)}, bf16[512,2,64]{0,2,1:T(8,128)(2,1)}, u32[]{:S(2)}, u32[]{:S(2)}) collective-permute-start(bf16[512,2,64]{0,2,1:T(8,128)(2,1)} %slice.176), channel_id=1, source_target_pairs={{1,0},{2,1},{3,2},{4,3},{5,4},{6,5},{7,6},{8,7},{9,8},{10,9},{11,1... | collective-permute-start | bytes 393224 | tf_op jit(solution)/shard_map/ppermute | solution.py:23
  394.5 40.3 %collective-permute-start.8 = (bf16[2,2,2,2,28,896]{5,3,4,2,1,0:T(2,128)(2,1)}, bf16[2,2,2,2,28,896]{5,3,4,2,1,0:T(2,128)(2,1)}, u32[]{:S(2)}, u32[]{:S(2)}) collective-permute-start(bf16[2,2,2,2,28,896]{5,3,4,2,1,0:T(2,128)(2,1)} %bitcast.273), channel_id=1, source_target_pairs={{0,1},{1,0},{2,3},{3,2},{4,5},{5,4},{6,7},{7,6},{8,9},{9,8},{10,11... | collective-permute-start | bytes 2408456 | tf_op jit(solution)/shard_map/ppermute | solution.py:86
  398.9 50.9 %collective-permute-start.5 = (bf16[2,2,2,152,896]{4,3,2,1,0:T(8,128)(2,1)}, bf16[2,2,2,152,896]{4,3,2,1,0:T(8,128)(2,1)}, u32[]{:S(2)}, u32[]{:S(2)}) collective-permute-start(bf16[2,2,2,152,896]{4,3,2,1,0:T(8,128)(2,1)} %dynamic-slice_bitcast_fusion.3), channel_id=1, source_target_pairs={{0,8},{1,9},{2,10},{3,11},{4,12},{5,13},{6,14},{7,15},{8,0},{9,1},... | collective-permute-start | bytes 6537224 | tf_op jit(solution)/shard_map/ppermute | solution.py:86
  410.9 49.8 %collective-permute-start.7 = (bf16[2,2,2,56,2432]{4,3,2,1,0:T(8,128)(2,1)}, bf16[2,2,2,56,2432]{4,3,2,1,0:T(8,128)(2,1)}, u32[]{:S(2)}, u32[]{:S(2)}) collective-permute-start(bf16[2,2,2,56,2432]{4,3,2,1,0:T(8,128)(2,1)} %dynamic-slice_bitcast_fusion.1), channel_id=1, source_target_pairs={{0,4},{1,5},{2,6},{3,7},{4,0},{5,1},{6,2},{7,3},{8,12},{9,13},{10,... | collective-permute-start | bytes 6537224 | tf_op jit(solution)/shard_map/ppermute | solution.py:86
  414.0 49.8 %collective-permute-start.6 = (bf16[2,2,2,56,2432]{4,3,2,1,0:T(8,128)(2,1)}, bf16[2,2,2,56,2432]{4,3,2,1,0:T(8,128)(2,1)}, u32[]{:S(2)}, u32[]{:S(2)}) collective-permute-start(bf16[2,2,2,56,2432]{4,3,2,1,0:T(8,128)(2,1)} %dynamic-slice_bitcast_fusion.2), channel_id=1, source_target_pairs={{0,2},{1,3},{2,0},{3,1},{4,6},{5,7},{6,4},{7,5},{8,10},{9,11},{10,... | collective-permute-start | bytes 6537224 | tf_op jit(solution)/shard_map/ppermute | solution.py:86
  466.9 31.7 %collective-permute-start.12 = (bf16[2,2,2,28,896]{4,3,2,1,0:T(8,128)(2,1)}, bf16[2,2,2,28,896]{4,3,2,1,0:T(8,128)(2,1)}, u32[]{:S(2)}, u32[]{:S(2)}) collective-permute-start(bf16[2,2,2,28,896]{4,3,2,1,0:T(8,128)(2,1)} %dynamic-slice_bitcast_fusion.11), channel_id=1, source_target_pairs={{0,4},{1,5},{2,6},{3,7},{4,0},{5,1},{6,2},{7,3},{8,12},{9,13},{10,... | collective-permute-start | bytes 1204232 | tf_op jit(solution)/shard_map/ppermute | solution.py:86
  471.5 28.5 %collective-permute-start.11 = (bf16[2,2,56,2432]{3,2,1,0:T(8,128)(2,1)}, bf16[2,2,56,2432]{3,2,1,0:T(8,128)(2,1)}, u32[]{:S(2)}, u32[]{:S(2)}) collective-permute-start(bf16[2,2,56,2432]{3,2,1,0:T(8,128)(2,1)} %dynamic-slice_bitcast_fusion.4), channel_id=1, source_target_pairs={{0,8},{1,9},{2,10},{3,11},{4,12},{5,13},{6,14},{7,15},{8,0},{9,1},... | collective-permute-start | bytes 3268616 | tf_op jit(solution)/shard_map/ppermute | solution.py:86
  472.0 30.4 %collective-permute-start.10 = (bf16[2,2,56,2432]{3,2,1,0:T(8,128)(2,1)}, bf16[2,2,56,2432]{3,2,1,0:T(8,128)(2,1)}, u32[]{:S(2)}, u32[]{:S(2)}) collective-permute-start(bf16[2,2,56,2432]{3,2,1,0:T(8,128)(2,1)} %dynamic-slice_bitcast_fusion.5), channel_id=1, source_target_pairs={{0,4},{1,5},{2,6},{3,7},{4,0},{5,1},{6,2},{7,3},{8,12},{9,13},{10,... | collective-permute-start | bytes 3268616 | tf_op jit(solution)/shard_map/ppermute | solution.py:86
  472.5 31.5 %collective-permute-start.9 = (bf16[2,2,152,896]{3,2,1,0:T(8,128)(2,1)}, bf16[2,2,152,896]{3,2,1,0:T(8,128)(2,1)}, u32[]{:S(2)}, u32[]{:S(2)}) collective-permute-start(bf16[2,2,152,896]{3,2,1,0:T(8,128)(2,1)} %dynamic-slice_bitcast_fusion.6), channel_id=1, source_target_pairs={{0,2},{1,3},{2,0},{3,1},{4,6},{5,7},{6,4},{7,5},{8,10},{9,11},{10,... | collective-permute-start | bytes 3268616 | tf_op jit(solution)/shard_map/ppermute | solution.py:86
  523.2 8.2 %collective-permute-start.13 = (bf16[512,2,64]{0,2,1:T(8,128)(2,1)S(1)}, bf16[512,2,64]{0,2,1:T(8,128)(2,1)S(1)}, u32[]{:S(2)}, u32[]{:S(2)}) collective-permute-start(bf16[512,2,64]{0,2,1:T(8,128)(2,1)S(1)} %slice.177), channel_id=1, source_target_pairs={{1,0},{2,1},{3,2},{4,3},{5,4},{6,5},{7,6},{8,7},{9,8},{10,9},{11,1... | collective-permute-start | bytes 393224 | tf_op jit(solution)/shard_map/ppermute | solution.py:23
  524.5 10.4 %collective-permute-start.18 = (bf16[2,2,28,896]{3,2,1,0:T(8,128)(2,1)S(1)}, bf16[2,2,28,896]{3,2,1,0:T(8,128)(2,1)S(1)}, u32[]{:S(2)}, u32[]{:S(2)}) collective-permute-start(bf16[2,2,28,896]{3,2,1,0:T(8,128)(2,1)S(1)} %dynamic-slice_bitcast_fusion.16), channel_id=1, source_target_pairs={{0,8},{1,9},{2,10},{3,11},{4,12},{5,13},{6,14},{7,15},{8,0},{9,1},... | collective-permute-start | bytes 602120 | tf_op jit(solution)/shard_map/ppermute | solution.py:86
  526.5 16.5 %collective-permute-start.17 = (bf16[2,56,2432]{2,1,0:T(8,128)(2,1)S(1)}, bf16[2,56,2432]{2,1,0:T(8,128)(2,1)S(1)}, u32[]{:S(2)}, u32[]{:S(2)}) collective-permute-start(bf16[2,56,2432]{2,1,0:T(8,128)(2,1)S(1)} %dynamic-slice_bitcast_fusion.8), channel_id=1, source_target_pairs={{0,2},{1,3},{2,0},{3,1},{4,6},{5,7},{6,4},{7,5},{8,10},{9,11},{10,... | collective-permute-start | bytes 1634312 | tf_op jit(solution)/shard_map/ppermute | solution.py:86
  527.8 14.2 %collective-permute-start.15 = (bf16[2,152,896]{2,1,0:T(8,128)(2,1)S(1)}, bf16[2,152,896]{2,1,0:T(8,128)(2,1)S(1)}, u32[]{:S(2)}, u32[]{:S(2)}) collective-permute-start(bf16[2,152,896]{2,1,0:T(8,128)(2,1)S(1)} %dynamic-slice_bitcast_fusion.10), channel_id=1, source_target_pairs={{0,4},{1,5},{2,6},{3,7},{4,0},{5,1},{6,2},{7,3},{8,12},{9,13},{10,... | collective-permute-start | bytes 1634312 | tf_op jit(solution)/shard_map/ppermute | solution.py:86
  529.1 16.6 %collective-permute-start.16 = (bf16[2,56,2432]{2,1,0:T(8,128)(2,1)S(1)}, bf16[2,56,2432]{2,1,0:T(8,128)(2,1)S(1)}, u32[]{:S(2)}, u32[]{:S(2)}) collective-permute-start(bf16[2,56,2432]{2,1,0:T(8,128)(2,1)S(1)} %dynamic-slice_bitcast_fusion.9), channel_id=1, source_target_pairs={{0,8},{1,9},{2,10},{3,11},{4,12},{5,13},{6,14},{7,15},{8,0},{9,1},... | collective-permute-start | bytes 1634312 | tf_op jit(solution)/shard_map/ppermute | solution.py:86
  553.9 14.8 %collective-permute-start.25 = (bf16[2,28,896]{2,1,0:T(8,128)(2,1)S(1)}, bf16[2,28,896]{2,1,0:T(8,128)(2,1)}, u32[]{:S(2)}, u32[]{:S(2)}) collective-permute-start(bf16[2,28,896]{2,1,0:T(8,128)(2,1)S(1)} %dynamic-slice_bitcast_fusion.18), channel_id=1, source_target_pairs={{0,2},{1,3},{2,0},{3,1},{4,6},{5,7},{6,4},{7,5},{8,10},{9,11},{10,... | collective-permute-start | bytes 301064 | tf_op jit(solution)/shard_map/ppermute | solution.py:86
  555.5 27.7 %collective-permute-start.24 = (bf16[56,2432]{1,0:T(8,128)(2,1)}, bf16[56,2432]{1,0:T(8,128)(2,1)}, u32[]{:S(2)}, u32[]{:S(2)}) collective-permute-start(bf16[56,2432]{1,0:T(8,128)(2,1)} %dynamic-slice_bitcast_fusion.13), channel_id=1, source_target_pairs={{0,16},{1,17},{2,18},{3,19},{4,20},{5,21},{6,22},{7,23},{8,24},{9,... | collective-permute-start | bytes 817160 | tf_op jit(solution)/shard_map/ppermute | solution.py:86
  558.0 31.1 %collective-permute-start.23 = (bf16[56,2432]{1,0:T(8,128)(2,1)}, bf16[56,2432]{1,0:T(8,128)(2,1)}, u32[]{:S(2)}, u32[]{:S(2)}) collective-permute-start(bf16[56,2432]{1,0:T(8,128)(2,1)} %dynamic-slice_bitcast_fusion.14), channel_id=1, source_target_pairs={{0,16},{1,17},{2,18},{3,19},{4,20},{5,21},{6,22},{7,23},{8,24},{9,... | collective-permute-start | bytes 817160 | tf_op jit(solution)/shard_map/ppermute | solution.py:86
  562.2 7.5 %collective-permute-start.19 = (bf16[2,2,2,2,29,1152]{5,3,4,2,1,0:T(2,128)(2,1)S(1)}, bf16[2,2,2,2,29,1152]{5,3,4,2,1,0:T(2,128)(2,1)S(1)}, u32[]{:S(2)}, u32[]{:S(2)}) collective-permute-start(bf16[2,2,2,2,29,1152]{5,3,4,2,1,0:T(2,128)(2,1)S(1)} %bitcast.311), channel_id=1, source_target_pairs={{0,1},{1,0},{2,3},{3,2},{4,5},{5,4},{6,7},{7,6},{8,9},{9,8},{10,11... | collective-permute-start | bytes 3207176 | tf_op jit(solution)/shard_map/ppermute | solution.py:86
  562.3 31.1 %collective-permute-start.22 = (bf16[152,896]{1,0:T(8,128)(2,1)S(1)}, bf16[152,896]{1,0:T(8,128)(2,1)S(1)}, u32[]{:S(2)}, u32[]{:S(2)}) collective-permute-start(bf16[152,896]{1,0:T(8,128)(2,1)S(1)} %dynamic-slice_bitcast_fusion.15), channel_id=1, source_target_pairs={{0,16},{1,17},{2,18},{3,19},{4,20},{5,21},{6,22},{7,23},{8,24},{9,... | collective-permute-start | bytes 817160 | tf_op jit(solution)/shard_map/ppermute | solution.py:86
  570.6 14.3 %collective-permute-start.20 = (bf16[2,2,2,29,1152]{4,2,3,1,0:T(2,128)(2,1)S(1)}, bf16[2,2,2,29,1152]{4,2,3,1,0:T(2,128)(2,1)S(1)}, u32[]{:S(2)}, u32[]{:S(2)}) collective-permute-start(bf16[2,2,2,29,1152]{4,2,3,1,0:T(2,128)(2,1)S(1)} %bitcast.317), channel_id=1, source_target_pairs={{0,2},{1,3},{2,0},{3,1},{4,6},{5,7},{6,4},{7,5},{8,10},{9,11},{10,... | collective-permute-start | bytes 1603592 | tf_op jit(solution)/shard_map/ppermute | solution.py:86
  585.1 8.5 %collective-permute-start.21 = (bf16[2,2,29,1152]{3,2,1,0:T(8,128)(2,1)S(1)}, bf16[2,2,29,1152]{3,2,1,0:T(8,128)(2,1)S(1)}, u32[]{:S(2)}, u32[]{:S(2)}) collective-permute-start(bf16[2,2,29,1152]{3,2,1,0:T(8,128)(2,1)S(1)} %dynamic-slice_bitcast_fusion.12), channel_id=1, source_target_pairs={{0,4},{1,5},{2,6},{3,7},{4,0},{5,1},{6,2},{7,3},{8,12},{9,13},{10,... | collective-permute-start | bytes 801800 | tf_op jit(solution)/shard_map/ppermute | solution.py:86
  594.3 9.7 %collective-permute-start.28 = (bf16[28,896]{1,0:T(8,128)(2,1)}, bf16[28,896]{1,0:T(8,128)(2,1)S(1)}, u32[]{:S(2)}, u32[]{:S(2)}) collective-permute-start(bf16[28,896]{1,0:T(8,128)(2,1)} %dynamic-slice_bitcast_fusion.20), channel_id=1, source_target_pairs={{0,16},{1,17},{2,18},{3,19},{4,20},{5,21},{6,22},{7,23},{8,24},{9,... | collective-permute-start | bytes 150536 | tf_op jit(solution)/shard_map/ppermute | solution.py:86
  594.4 7.5 %collective-permute-start.26 = (bf16[2,29,1152]{2,1,0:T(8,128)(2,1)S(1)}, bf16[2,29,1152]{2,1,0:T(8,128)(2,1)}, u32[]{:S(2)}, u32[]{:S(2)}) collective-permute-start(bf16[2,29,1152]{2,1,0:T(8,128)(2,1)S(1)} %dynamic-slice_bitcast_fusion.17), channel_id=1, source_target_pairs={{0,8},{1,9},{2,10},{3,11},{4,12},{5,13},{6,14},{7,15},{8,0},{9,1},... | collective-permute-start | bytes 400904 | tf_op jit(solution)/shard_map/ppermute | solution.py:86
  599.9 10.1 %collective-permute-start.29 = (f32[28,4864]{1,0:T(8,128)}, f32[28,4864]{1,0:T(8,128)S(1)}, u32[]{:S(2)}, u32[]{:S(2)}) collective-permute-start(f32[28,4864]{1,0:T(8,128)} %dynamic-slice_bitcast_fusion.7), channel_id=1, source_target_pairs={{0,1},{1,0},{2,3},{3,2},{4,5},{5,4},{6,7},{7,6},{8,9},{9,8},{10,11... | collective-permute-start | bytes 1634312 | tf_op jit(solution)/shard_map/ppermute | solution.py:86
  602.9 5.3 collective-permute-start.27
  (72 other events, 836.3 us)
Sparse Core Ops, SparseCore 0:
  11.5 63.2 all-gather.3
  80.1 118.2 all-gather.5
  202.0 76.7 all-gather.7
